TPU v7x, 32 devices: a whole 2x2x4 slice. The times are simulated.
32 devices in a mesh: sec: 2 (over core), grp: 16 (over z, y, x).
Axes of the slice: x: 2, y: 2, z: 4, core: 2. Of those that a mesh axis runs over, the one named last changes fastest.
Arguments:
- stratum_warmth_anomaly: float32 [90, 8192], P('sec', 'grp'), may hold values from 0.7 to 1.3
- pressure_depth: float32 [90, 8192], P('sec', 'grp'), may hold values from 0.5 to 2
- absorber_amounts: float32 [4, 90, 8192], P(None, 'sec', 'grp'), may hold values from 0.1 to 1
- ground_warmth_anomaly: float32 [8192], P('grp'), may hold values from 0.9 to 1.3
- sun_elevation_factor: float32 [8192], P('grp'), may hold values from 0.2 to 1
- daytime_mask: int32 [8192], P('grp'), may hold values 0 or 1
- dispatch_position: int32 [16, 512], P('grp'), may hold values from 0 to 511, each once within a row
- arrival_membership: int32 [16, 512], P('grp'), may hold values from 0 to 511, each once within a row
- adjacency_table: int32 [6, 8192], P(None, 'grp'), may hold values from 0 to 639, as said below
- blending_coefficient: float32 [6, 8192], P(None, 'grp'), may hold values from 0.02 to 0.15
- opacity_table: float32 [4, 112, 90], P(None, 'sec'), may hold values from 0.001 to 0.3
- emission_share: float32 [112], P('sec'), may hold values from 0.05 to 0.5
- sunshine_share: float32 [112], P('sec'), may hold values from 0.05 to 0.5
Outputs:
- heating: float32 [90, 8192], P('sec', 'grp')
- mixed: float32 [4, 90, 8192], P(None, 'sec', 'grp')
Inputs may be any that keep to these rules, and one draw needn't show every extreme that they name: `dispatch_position`: each row is a permutation of 0 to 511. `arrival_membership`: each row is a permutation of 0 to 511, so every radiation column has exactly four members. adjacency_table[k, c] - (c mod 512) lies in 0 to 128.
All inputs are finite; a program needn't handle non-finite values. No bound on the sum of `daytime_mask` on one device may be relied on, other than what follows from the above.
Results may differ from a plain program's by a relative error of at most 0.0003.
Values sent between devices are 32-bit elements; how exact they have to be, the bound alone decides.
A program may use at most 64 MiB of HBM per device.

v0:
```python
import jax
import jax.numpy as jnp
from jax import lax
from jax.sharding import PartitionSpec as P

STEPS = 4
LEVEL_BLOCK = 9
HALO = 64


DIFFUSE = 1.66
TOP = lax.Precision.HIGHEST


def padded(shard, sides, width):
    for axis, dim in sides:
        size, length = (lax.axis_size(axis), shard.shape[dim])
        up = [(i, (i + 1) % size) for i in range(size)]
        down = [(j, i) for i, j in up]
        last = lax.slice_in_dim(shard, length - width, length, axis=dim)
        first = lax.slice_in_dim(shard, 0, width, axis=dim)
        before = lax.ppermute(last, axis, up)
        after = lax.ppermute(first, axis, down)
        shard = jnp.concatenate([before, shard, after], axis=dim)
    return shard


def select_matrix(ids, count):
    return (ids[:, None] == jnp.arange(count, dtype=jnp.int32)[None, :]).astype(jnp.float32)


def pick_columns(values, selector):
    return lax.dot_general(values, selector, (((1,), (1,)), ((), ())), precision=TOP)


def optical(level_table, radiant_species, stratum_index):
    coeffs = lax.dynamic_index_in_dim(level_table, stratum_index, 0, keepdims=False)
    amounts = lax.dynamic_index_in_dim(radiant_species, stratum_index, 1, keepdims=False)
    optical_depth = coeffs[0][:, None] * amounts[0][None, :]
    for species in range(1, coeffs.shape[0]):
        optical_depth = optical_depth + coeffs[species][:, None] * amounts[species][None, :]
    return optical_depth


def compute_flux_heating(
    radiant_warmth,
    radiant_depth,
    radiant_species,
    radiant_ground,
    sunlight_incline,
    incoming_sunshine,
    opacity_table,
    emission_share,
    sunshine_share,
):
    strata_range, radiant_span = radiant_warmth.shape
    blocks = strata_range // LEVEL_BLOCK
    gpoints = emission_share.shape[0]
    block_ids = jnp.arange(blocks, dtype=jnp.int32)
    level_table = jnp.transpose(opacity_table, (2, 0, 1))

    def layer_terms(stratum_index):
        optical_depth = optical(level_table, radiant_species, stratum_index)
        stratum_warmth = lax.dynamic_index_in_dim(radiant_warmth, stratum_index, 0, keepdims=False)
        source = emission_share[:, None] * (stratum_warmth**4)[None, :]
        return (optical_depth, jnp.exp(-DIFFUSE * optical_depth), source)

    def down_block(fluxes, block_id):
        thermal, direct = fluxes
        thermal_rows = []
        direct_rows = []
        for inner_id in range(LEVEL_BLOCK):
            optical_depth, transmit, source = layer_terms(block_id * LEVEL_BLOCK + inner_id)
            thermal = transmit * thermal + (1.0 - transmit) * source
            direct = direct * jnp.exp(-optical_depth / sunlight_incline[None, :])
            thermal_rows.append(jnp.sum(thermal, axis=0))
            direct_rows.append(jnp.sum(direct, axis=0))
        return ((thermal, direct), (jnp.stack(thermal_rows), jnp.stack(direct_rows)))

    down_init = (
        jnp.zeros((gpoints, radiant_span), jnp.float32),
        sunshine_share[:, None] * incoming_sunshine[None, :],
    )
    final_down, (down_rows, direct_rows) = lax.scan(down_block, down_init, block_ids)
    thermal_down = jnp.concatenate(
        [jnp.zeros((1, radiant_span), jnp.float32), down_rows.reshape(strata_range, radiant_span)],
        axis=0,
    )
    direct_down = jnp.concatenate(
        [jnp.sum(down_init[1], axis=0)[None], direct_rows.reshape(strata_range, radiant_span)],
        axis=0,
    )

    def up_block(upward, block_id):
        upward_rows = []
        for inner_id in range(LEVEL_BLOCK - 1, -1, -1):
            optical_depth, transmit, source = layer_terms(block_id * LEVEL_BLOCK + inner_id)
            upward = transmit * upward + (1.0 - transmit) * source
            upward_rows.append(jnp.sum(upward, axis=0))
        return (upward, jnp.stack(upward_rows[::-1]))

    up_init = emission_share[:, None] * (radiant_ground**4)[None, :]
    final_up, up_rows = lax.scan(up_block, up_init, block_ids, reverse=True)
    upward_flux = jnp.concatenate(
        [up_rows.reshape(strata_range, radiant_span), jnp.sum(up_init, axis=0)[None]], axis=0
    )
    net_flux = thermal_down - upward_flux + direct_down
    return (net_flux[:-1] - net_flux[1:]) / radiant_depth


def per_device(
    stratum_warmth_anomaly,
    pressure_depth,
    absorber_amounts,
    ground_warmth_anomaly,
    sun_elevation_factor,
    daytime_mask,
    dispatch_position,
    arrival_membership,
    adjacency_table,
    blending_coefficient,
    opacity_table,
    emission_share,
    sunshine_share,
):
    cell_sequence = stratum_warmth_anomaly.shape[1]
    position = dispatch_position[0]
    placing = select_matrix(position, cell_sequence)
    state_bundle = jnp.concatenate(
        [stratum_warmth_anomaly[None], pressure_depth[None], absorber_amounts], axis=0
    )
    surface = jnp.stack(
        [
            ground_warmth_anomaly,
            sun_elevation_factor,
            daytime_mask.astype(jnp.float32) * sun_elevation_factor,
        ],
        axis=0,
    )[:, None, :]
    packed = jnp.dot(state_bundle.reshape(-1, cell_sequence), placing, precision=TOP).reshape(
        state_bundle.shape
    )
    packed_surface = jnp.dot(surface.reshape(3, cell_sequence), placing, precision=TOP).reshape(
        surface.shape
    )
    groups_dev = cell_sequence // 4
    group_ids = arrival_membership[0] // 4
    half_arrived, arrived_surface = (
        lax.all_to_all(packed, "grp", split_axis=2, concat_axis=2, tiled=True),
        lax.all_to_all(packed_surface, "grp", split_axis=2, concat_axis=2, tiled=True),
    )
    arrived = lax.all_gather(half_arrived, "sec", axis=1, tiled=True)
    selector = select_matrix(group_ids, groups_dev)
    member = selector * 0.25
    flattened = arrived.reshape(-1, cell_sequence)
    pooled = jnp.dot(flattened, member, precision=TOP).reshape(
        arrived.shape[0], arrived.shape[1], groups_dev
    )
    pooled_surface = jnp.dot(arrived_surface.reshape(3, cell_sequence), member, precision=TOP)
    heat_part = compute_flux_heating(
        pooled[0],
        pooled[1],
        pooled[2:],
        pooled_surface[0],
        pooled_surface[1],
        pooled_surface[2],
        opacity_table,
        emission_share,
        sunshine_share,
    )
    slot_heat = pick_columns(heat_part, selector)
    returned = lax.all_to_all(slot_heat, "grp", split_axis=1, concat_axis=1, tiled=True)
    own_heat = pick_columns(returned, placing)
    heating = lax.psum_scatter(own_heat, "sec", scatter_dimension=0, tiled=True)
    extended_span = cell_sequence + 2 * HALO
    source_rows = jnp.arange(extended_span, dtype=jnp.int32)[:, None]
    blend_matrix = jnp.zeros((extended_span, cell_sequence), jnp.float32)
    for near_id in range(adjacency_table.shape[0]):
        blend_matrix = blend_matrix + jnp.where(
            adjacency_table[near_id][None, :] == source_rows,
            blending_coefficient[near_id][None, :],
            0.0,
        )
    centre_rows = jnp.arange(cell_sequence, dtype=jnp.int32)[None, :] + HALO
    weight_total = jnp.sum(blending_coefficient, axis=0)
    blend_matrix = blend_matrix - jnp.where(source_rows == centre_rows, weight_total[None, :], 0.0)
    mixed = absorber_amounts
    for step_id in range(STEPS):
        extended = padded(mixed, (("grp", 2),), HALO)
        update = jnp.dot(extended.reshape(-1, extended_span), blend_matrix, precision=TOP).reshape(
            mixed.shape
        )
        mixed = mixed + update
    return (heating, mixed)


def solution(mesh):
    in_specs = (
        P("sec", "grp"),
        P("sec", "grp"),
        P(None, "sec", "grp"),
        P("grp"),
        P("grp"),
        P("grp"),
        P("grp", None),
        P("grp", None),
        P(None, "grp"),
        P(None, "grp"),
        P(None, "sec", None),
        P("sec"),
        P("sec"),
    )
    out_specs = (P("sec", "grp"), P(None, "sec", "grp"))
    return jax.shard_map(
        per_device, mesh=mesh, in_specs=in_specs, out_specs=out_specs, check_vma=False
    )
```

profile of v0, /device:TPU:0, one launch (start us, length us, event | category | flops | bytes accessed | tf_op | source)
XLA Modules:
  0.0 178.2 jit_solution(6171241236418006057)
XLA Ops:
  7.9 2.5 %fusion.150 = f32[3,512]{0,1:T(8,128)} fusion(s32[512]{0:T(512)} %bitcast.552, f32[1,512]{1,0:T(1,128)S(1)} %bitcast.606, f32[1,512]{1,0:T(1,128)} %bitcast.557, f32[1,512]{1,0:T(1,128)} %bitcast.610), kind=kOutput, calls=%fused_computation.369 | convolution fusion | flops 9702400 | bytes 14336 | tf_op jit(solution)/shard_map/dot_general | solution.py:143
  10.4 8.3 %all-to-all-start = ((f32[3,1,512]{0,1,2:T(1,128)}), f32[3,1,512]{0,1,2:T(1,128)S(1)}, u32[]{:S(2)}, u32[]{:S(2)}) async-start(f32[3,1,512]{0,1,2:T(1,128)} %bitcast.226), calls=%async_computation | async-start | bytes 524288 | tf_op jit(solution)/shard_map/all_to_all | solution.py:150
  18.8 1.1 copy.43
  20.0 5.6 %collective-permute-start.1 = (f32[4,45,64]{2,1,0:T(8,128)S(1)}, f32[4,45,64]{2,1,0:T(8,128)}, u32[]{:S(2)}, u32[]{:S(2)}) collective-permute-start(f32[4,45,64]{2,1,0:T(8,128)S(1)} %get-tuple-element.643), channel_id=1, source_target_pairs={{1,0},{2,1},{3,2},{4,3},{5,4},{6,5},{7,6},{8,7},{9,8},{10,9},{11,1... | collective-permute-start | bytes 138248 | tf_op jit(solution)/shard_map/ppermute | solution.py:23
  25.6 1.6 fusion.151
  27.2 1.9 %copy.44 = f32[6,45,512]{1,0,2:T(8,128)S(1)} copy(f32[6,45,512]{2,1,0:T(8,128)} %fusion.151) | data formatting | bytes 1105920 | tf_op jit(solution)/shard_map/dot_general | solution.py:140
  29.1 2.9 %reshape.462 = f32[16,1,8640]{2,1,0:T(1,128)} reshape(f32[512,6,45]{2,1,0:T(8,128)S(1)} %bitcast.519) | data formatting | bytes 1105920
  32.0 7.1 %all-to-all-start.1 = ((f32[16,1,8640]{2,1,0:T(1,128)}), f32[16,1,8640]{2,1,0:T(1,128)S(1)}, u32[]{:S(2)}, u32[]{:S(2)}) async-start(f32[16,1,8640]{2,1,0:T(1,128)} %reshape.462), calls=%async_computation.1 | async-start | bytes 1114112 | tf_op jit(solution)/shard_map/all_to_all | solution.py:149
  41.5 12.4 %all-to-all-done.1 = f32[16,1,8640]{2,1,0:T(1,128)S(1)} async-done(((f32[16,1,8640]{2,1,0:T(1,128)}), f32[16,1,8640]{2,1,0:T(1,128)S(1)}, u32[]{:S(2)}, u32[]{:S(2)}) %all-to-all-start.1) | async-done | bytes 552992 | tf_op jit(solution)/shard_map/all_to_all | solution.py:149
  54.4 2.0 %reduce = f32[16,8640]{1,0:T(8,128)S(1)} reduce(f32[16,1,8640]{2,1,0:T(1,128)S(1)} %all-to-all-done.1, f32[]{:T(128)} %broadcast.174), dimensions={1}, to_apply=%all_to_all.15.reduce_sub_computation | reduce | bytes 1105924 | tf_op jit(solution)/shard_map/all_to_all | solution.py:149
  56.4 1.4 reshape.463
  57.8 1.8 %copy.45 = f32[6,45,512]{2,0,1:T(8,128)} copy(f32[6,45,512]{1,0,2:T(8,128)S(1)} %bitcast.520) | data formatting | bytes 1105920 | tf_op jit(solution)/shard_map/all_to_all | solution.py:149
  59.7 3.3 %fusion.136 = f32[4,45,512]{2,1,0:T(8,128)S(1)} fusion(f32[4,45,512]{2,1,0:T(8,128)S(1)} %copy.43, f32[4,45,64]{2,1,0:T(8,128)} %collective-permute-done.1, f32[4,45,64]{2,1,0:T(8,128)} %collective-permute-done, f32[512]{0:T(512)S(1)} %reduce_sum.380, s32[512]{0:T(512)S(1)} %iota_add_fusion, f32[512]{0:T(512)S(1)} %bitcast.578, s32[512]{0:T(512)S(1)} %bitcast.598, ...), kind=kOutput, calls=%fused_computation.362 | convolution fusion | flops 714664960 | bytes 858112 | tf_op jit(solution)/shard_map/dot_general | solution.py:190
  63.0 2.6 %collective-permute-start.3 = (f32[4,45,64]{2,1,0:T(8,128)S(1)}, f32[4,45,64]{2,1,0:T(8,128)S(1)}, u32[]{:S(2)}, u32[]{:S(2)}) collective-permute-start(f32[4,45,64]{2,1,0:T(8,128)S(1)} %get-tuple-element.641), channel_id=1, source_target_pairs={{1,0},{2,1},{3,2},{4,3},{5,4},{6,5},{7,6},{8,7},{9,8},{10,9},{11,1... | collective-permute-start | bytes 138248 | tf_op jit(solution)/shard_map/ppermute | solution.py:23
  65.7 2.1 %collective-permute-done.3 = f32[4,45,64]{2,1,0:T(8,128)S(1)} collective-permute-done((f32[4,45,64]{2,1,0:T(8,128)S(1)}, f32[4,45,64]{2,1,0:T(8,128)S(1)}, u32[]{:S(2)}, u32[]{:S(2)}) %collective-permute-start.3) | collective-permute-done | bytes 46112 | tf_op jit(solution)/shard_map/ppermute | solution.py:23
  67.8 6.1 %collective-permute-done.2 = f32[4,45,64]{2,1,0:T(8,128)S(1)} collective-permute-done((f32[4,45,64]{2,1,0:T(8,128)S(1)}, f32[4,45,64]{2,1,0:T(8,128)S(1)}, u32[]{:S(2)}, u32[]{:S(2)}) %collective-permute-start.2) | collective-permute-done | bytes 46112 | tf_op jit(solution)/shard_map/ppermute | solution.py:22
  74.0 2.3 %fusion.139 = f32[4,45,512]{2,1,0:T(8,128)S(1)} fusion(f32[4,45,512]{2,1,0:T(8,128)S(1)} %fusion.136, f32[4,45,64]{2,1,0:T(8,128)S(1)} %collective-permute-done.3, f32[4,45,64]{2,1,0:T(8,128)S(1)} %collective-permute-done.2, f32[512]{0:T(512)S(1)} %reduce_sum.380, s32[512]{0:T(512)S(1)} %iota_add_fusion, f32[512]{0:T(512)S(1)} %bitcast.579, ...), kind=kOutput, calls=%fused_computation.363 | convolution fusion | flops 714664960 | bytes 858112 | tf_op jit(solution)/shard_map/dot_general | solution.py:190
  77.0 2.0 %collective-permute-start.4 = (f32[4,45,64]{2,1,0:T(8,128)S(1)}, f32[4,45,64]{2,1,0:T(8,128)}, u32[]{:S(2)}, u32[]{:S(2)}) collective-permute-start(f32[4,45,64]{2,1,0:T(8,128)S(1)} %get-tuple-element.638), channel_id=1, source_target_pairs={{0,1},{1,2},{2,3},{3,4},{4,5},{5,6},{6,7},{7,8},{8,9},{9,10},{10,1... | collective-permute-start | bytes 138248 | tf_op jit(solution)/shard_map/ppermute | solution.py:22
  79.1 2.0 %copy.46 = f32[6,90,512]{2,1,0:T(8,128)S(1)} copy(f32[6,90,512]{2,0,1:T(8,128)} %all-gather.2.cloned.1.call-done) | data formatting | bytes 2211840 | tf_op jit(solution)/shard_map/all_gather | solution.py:152
  81.2 1.1 fusion.181
  82.4 28.4 %while.35 = (s32[]{:T(128)}, f32[56,128]{1,0:T(8,128)S(1)}, f32[10,9,128]{2,1,0:T(8,128)S(1)}, s32[10]{0:T(128)S(1)}, f32[90,4,56]{2,1,0:T(4,128)S(1)}, /*index=...) while((s32[]{:T(128)}, f32[56,128]{1,0:T(8,128)S(1)}, ...), condition=%wide.region_30.31_spmd, body=%wide.region_20.30_spmd.sunk | while | flops 904362 | bytes 658635 | solution.py:103
  110.9 32.8 %while.36 = (s32[]{:T(128)}, f32[56,128]{1,0:T(8,128)S(1)}, f32[56,128]{1,0:T(8,128)S(1)}, f32[10,9,128]{2,1,0:T(8,128)S(1)}, f32[10,9,128]{2,1,0:T(8,128)S(1)},...) while((s32[]{:T(128)}, f32[56,128]{1,0:T(8,128)S(1)}, ...), condition=%wide.region_19.20_spmd.clone, body=%wide.region_0.19_spmd.clone.sunk | while | flops 1620010 | bytes 1230241 | solution.py:84
  143.9 1.0 fusion.185
  144.9 5.0 %all-to-all-start.2 = ((f32[90,16,32]{0,2,1:T(8,128)}), f32[90,16,32]{0,2,1:T(8,128)S(1)}, u32[]{:S(2)}, u32[]{:S(2)}) async-start(f32[90,16,32]{0,2,1:T(8,128)} %bitcast.107), calls=%async_computation.2 | async-start | bytes 524288 | tf_op jit(solution)/shard_map/all_to_all | solution.py:172
  150.0 3.3 %fusion.142 = f32[4,45,512]{2,1,0:T(8,128)S(1)} fusion(f32[4,45,512]{2,1,0:T(8,128)S(1)} %fusion.139, f32[4,45,64]{2,1,0:T(8,128)} %collective-permute-done.5, f32[4,45,64]{2,1,0:T(8,128)} %collective-permute-done.4, f32[512]{0:T(512)S(1)} %copy-done.6, s32[512]{0:T(512)S(1)} %copy-done.33, f32[512]{0:T(512)S(1)} %bitcast.580, s32[512]{0:T(512)S(1)} %bitcast.600, ...), kind=kOutput, calls=%fused_computation.364 | convolution fusion | flops 714664960 | bytes 858112 | tf_op jit(solution)/shard_map/dot_general | solution.py:190
  153.4 5.6 %collective-permute-start.7 = (f32[4,45,64]{2,1,0:T(8,128)S(1)}, f32[4,45,64]{2,1,0:T(8,128)S(1)}, u32[]{:S(2)}, u32[]{:S(2)}) collective-permute-start(f32[4,45,64]{2,1,0:T(8,128)S(1)} %get-tuple-element.637), channel_id=1, source_target_pairs={{1,0},{2,1},{3,2},{4,3},{5,4},{6,5},{7,6},{8,7},{9,8},{10,9},{11,1... | collective-permute-start | bytes 138248 | tf_op jit(solution)/shard_map/ppermute | solution.py:23
  159.0 0.8 fusion.148
  159.8 3.0 %fusion = f32[48,512]{1,0:T(8,128)S(1)} fusion(f32[90,512]{1,0:T(8,128)S(1)} %fusion.148), kind=kCustom, calls=%all-reduce-scatter | all-reduce-scatter fusion | flops 49153 | bytes 283136
  162.8 2.5 %collective-permute-start.8 = (f32[3,512]{1,0:T(4,128)S(1)}, f32[3,512]{1,0:T(4,128)S(1)}, u32[]{:S(2)}, u32[]{:S(2)}) collective-permute-start(f32[3,512]{1,0:T(4,128)S(1)} %slice.1427), channel_id=1, source_target_pairs={{0,16},{1,17},{2,18},{3,19},{4,20},{5,21},{6,22},{7,23},{8,24},{9,... | collective-permute-start | bytes 18440
  165.3 1.9 %collective-permute-done.6 = f32[4,45,64]{2,1,0:T(8,128)S(1)} collective-permute-done((f32[4,45,64]{2,1,0:T(8,128)S(1)}, f32[4,45,64]{2,1,0:T(8,128)S(1)}, u32[]{:S(2)}, u32[]{:S(2)}) %collective-permute-start.6) | collective-permute-done | bytes 46112 | tf_op jit(solution)/shard_map/ppermute | solution.py:22
  167.2 2.3 %fusion.145 = f32[4,45,512]{2,1,0:T(8,128)S(1)} fusion(f32[4,45,512]{2,1,0:T(8,128)S(1)} %fusion.142, f32[4,45,64]{2,1,0:T(8,128)S(1)} %collective-permute-done.7, f32[4,45,64]{2,1,0:T(8,128)S(1)} %collective-permute-done.6, f32[512]{0:T(512)S(1)} %copy-done.6, s32[512]{0:T(512)S(1)} %copy-done.33, f32[512]{0:T(512)S(1)} %bitcast.581, ...), kind=kOutput, calls=%fused_computation.365 | convolution fusion | flops 714664960 | bytes 858112 | tf_op jit(solution)/shard_map/dot_general | solution.py:190
  169.5 1.0 copy.52
  (664 shorter events, 50.4 us)
Async XLA Ops:
  7.2 18.4 %copy-start.4 = (s32[1,512]{1,0:T(1,128)S(1)}, s32[1,512]{1,0:T(1,128)}, u32[]{:S(2)}) copy-start(s32[1,512]{1,0:T(1,128)} %param.23) | copy-start | bytes 6148
  7.2 18.4 %copy-start.36 = (f32[45,512]{1,0:T(8,128)S(1)}, f32[45,512]{1,0:T(8,128)}, u32[]{:S(2)}) copy-start(f32[45,512]{1,0:T(8,128)} %param.18) | copy-start | bytes 276484
  7.2 18.4 %copy-start.37 = (f32[45,512]{1,0:T(8,128)S(1)}, f32[45,512]{1,0:T(8,128)}, u32[]{:S(2)}) copy-start(f32[45,512]{1,0:T(8,128)} %param.17) | copy-start | bytes 276484
  10.4 21.6 %all-to-all-start = ((f32[3,1,512]{0,1,2:T(1,128)}), f32[3,1,512]{0,1,2:T(1,128)S(1)}, u32[]{:S(2)}, u32[]{:S(2)}) async-start(f32[3,1,512]{0,1,2:T(1,128)} %bitcast.226), calls=%async_computation | async-start | bytes 524288 | tf_op jit(solution)/shard_map/all_to_all | solution.py:150
  20.0 39.6 %collective-permute-start.1 = (f32[4,45,64]{2,1,0:T(8,128)S(1)}, f32[4,45,64]{2,1,0:T(8,128)}, u32[]{:S(2)}, u32[]{:S(2)}) collective-permute-start(f32[4,45,64]{2,1,0:T(8,128)S(1)} %get-tuple-element.643), channel_id=1, source_target_pairs={{1,0},{2,1},{3,2},{4,3},{5,4},{6,5},{7,6},{8,7},{9,8},{10,9},{11,1... | collective-permute-start | bytes 138248 | tf_op jit(solution)/shard_map/ppermute | solution.py:23
  25.5 34.1 %collective-permute-start = (f32[4,45,64]{2,1,0:T(8,128)S(1)}, f32[4,45,64]{2,1,0:T(8,128)}, u32[]{:S(2)}, u32[]{:S(2)}) collective-permute-start(f32[4,45,64]{2,1,0:T(8,128)S(1)} %get-tuple-element.642), channel_id=1, source_target_pairs={{0,1},{1,2},{2,3},{3,4},{4,5},{5,6},{6,7},{7,8},{8,9},{9,10},{10,1... | collective-permute-start | bytes 138248 | tf_op jit(solution)/shard_map/ppermute | solution.py:22
  29.1 10.1 %copy-start.31 = (s32[1,512]{1,0:T(1,128)S(1)}, s32[1,512]{1,0:T(1,128)}, u32[]{:S(2)}) copy-start(s32[1,512]{1,0:T(1,128)} %param.24) | copy-start | bytes 6148
  29.1 10.2 %copy-start.1 = (f32[4,56,90]{2,1,0:T(8,128)S(1)}, f32[4,56,90]{2,1,0:T(8,128)}, u32[]{:S(2)}) copy-start(f32[4,56,90]{2,1,0:T(8,128)} %param.27) | copy-start | bytes 241924
  32.0 21.8 %all-to-all-start.1 = ((f32[16,1,8640]{2,1,0:T(1,128)}), f32[16,1,8640]{2,1,0:T(1,128)S(1)}, u32[]{:S(2)}, u32[]{:S(2)}) async-start(f32[16,1,8640]{2,1,0:T(1,128)} %reshape.462), calls=%async_computation.1 | async-start | bytes 1114112 | tf_op jit(solution)/shard_map/all_to_all | solution.py:149
  39.2 39.9 %all-gather.2.cloned.1.call-start = ((), (), s32[]{:S(2)}) async-start(), calls=%async_computation.3 | async-start | bytes 2211840 | tf_op jit(solution)/shard_map/all_gather | solution.py:152
  40.7 33.2 %copy-start.5 = (f32[512]{0:T(512)}, f32[512]{0:T(512)S(1)}, u32[]{:S(2)}) copy-start(f32[512]{0:T(512)S(1)} %reduce_sum.380) | copy-start | bytes 6148
  40.7 33.2 %copy-start.32 = (s32[512]{0:T(512)}, s32[512]{0:T(512)S(1)}, u32[]{:S(2)}) copy-start(s32[512]{0:T(512)S(1)} %iota_add_fusion) | copy-start | bytes 6148
  40.7 33.2 %copy-start.7 = (f32[1,512]{1,0:T(1,128)}, f32[1,512]{1,0:T(1,128)S(1)}, u32[]{:S(2)}) copy-start(f32[1,512]{1,0:T(1,128)S(1)} %get-tuple-element.650) | copy-start | bytes 6148
  40.8 33.2 %copy-start.9 = (f32[1,512]{1,0:T(1,128)}, f32[1,512]{1,0:T(1,128)S(1)}, u32[]{:S(2)}) copy-start(f32[1,512]{1,0:T(1,128)S(1)} %get-tuple-element.651) | copy-start | bytes 6148
  40.8 33.2 %copy-start.11 = (f32[1,512]{1,0:T(1,128)}, f32[1,512]{1,0:T(1,128)S(1)}, u32[]{:S(2)}) copy-start(f32[1,512]{1,0:T(1,128)S(1)} %get-tuple-element.652) | copy-start | bytes 6148
  40.8 33.2 %copy-start.13 = (f32[1,512]{1,0:T(1,128)}, f32[1,512]{1,0:T(1,128)S(1)}, u32[]{:S(2)}) copy-start(f32[1,512]{1,0:T(1,128)S(1)} %get-tuple-element.653) | copy-start | bytes 6148
  40.8 33.2 %copy-start.15 = (f32[1,512]{1,0:T(1,128)}, f32[1,512]{1,0:T(1,128)S(1)}, u32[]{:S(2)}) copy-start(f32[1,512]{1,0:T(1,128)S(1)} %get-tuple-element.654) | copy-start | bytes 6148
  40.8 33.2 %copy-start.17 = (f32[1,512]{1,0:T(1,128)}, f32[1,512]{1,0:T(1,128)S(1)}, u32[]{:S(2)}) copy-start(f32[1,512]{1,0:T(1,128)S(1)} %get-tuple-element.655) | copy-start | bytes 6148
  40.8 33.1 %copy-start.19 = (s32[1,512]{1,0:T(1,128)}, s32[1,512]{1,0:T(1,128)S(1)}, u32[]{:S(2)}) copy-start(s32[1,512]{1,0:T(1,128)S(1)} %get-tuple-element.644) | copy-start | bytes 6148
  40.8 33.1 %copy-start.21 = (s32[1,512]{1,0:T(1,128)}, s32[1,512]{1,0:T(1,128)S(1)}, u32[]{:S(2)}) copy-start(s32[1,512]{1,0:T(1,128)S(1)} %get-tuple-element.645) | copy-start | bytes 6148
  40.8 33.1 %copy-start.23 = (s32[1,512]{1,0:T(1,128)}, s32[1,512]{1,0:T(1,128)S(1)}, u32[]{:S(2)}) copy-start(s32[1,512]{1,0:T(1,128)S(1)} %get-tuple-element.646) | copy-start | bytes 6148
  40.9 33.1 %copy-start.25 = (s32[1,512]{1,0:T(1,128)}, s32[1,512]{1,0:T(1,128)S(1)}, u32[]{:S(2)}) copy-start(s32[1,512]{1,0:T(1,128)S(1)} %get-tuple-element.647) | copy-start | bytes 6148
  40.9 33.1 %copy-start.27 = (s32[1,512]{1,0:T(1,128)}, s32[1,512]{1,0:T(1,128)S(1)}, u32[]{:S(2)}) copy-start(s32[1,512]{1,0:T(1,128)S(1)} %get-tuple-element.648) | copy-start | bytes 6148
  40.9 33.1 %copy-start.29 = (s32[1,512]{1,0:T(1,128)}, s32[1,512]{1,0:T(1,128)S(1)}, u32[]{:S(2)}) copy-start(s32[1,512]{1,0:T(1,128)S(1)} %get-tuple-element.649) | copy-start | bytes 6148
  63.0 4.8 %collective-permute-start.3 = (f32[4,45,64]{2,1,0:T(8,128)S(1)}, f32[4,45,64]{2,1,0:T(8,128)S(1)}, u32[]{:S(2)}, u32[]{:S(2)}) collective-permute-start(f32[4,45,64]{2,1,0:T(8,128)S(1)} %get-tuple-element.641), channel_id=1, source_target_pairs={{1,0},{2,1},{3,2},{4,3},{5,4},{6,5},{7,6},{8,7},{9,8},{10,9},{11,1... | collective-permute-start | bytes 138248 | tf_op jit(solution)/shard_map/ppermute | solution.py:23
  65.6 8.3 %collective-permute-start.2 = (f32[4,45,64]{2,1,0:T(8,128)S(1)}, f32[4,45,64]{2,1,0:T(8,128)S(1)}, u32[]{:S(2)}, u32[]{:S(2)}) collective-permute-start(f32[4,45,64]{2,1,0:T(8,128)S(1)} %get-tuple-element.640), channel_id=1, source_target_pairs={{0,1},{1,2},{2,3},{3,4},{4,5},{5,6},{6,7},{7,8},{8,9},{9,10},{10,1... | collective-permute-start | bytes 138248 | tf_op jit(solution)/shard_map/ppermute | solution.py:22
  77.0 72.8 %collective-permute-start.5 = (f32[4,45,64]{2,1,0:T(8,128)}, f32[4,45,64]{2,1,0:T(8,128)}, u32[]{:S(2)}, u32[]{:S(2)}) collective-permute-start(f32[4,45,64]{2,1,0:T(8,128)} %get-tuple-element.639), channel_id=1, source_target_pairs={{1,0},{2,1},{3,2},{4,3},{5,4},{6,5},{7,6},{8,7},{9,8},{10,9},{11,1... | collective-permute-start | bytes 138248 | tf_op jit(solution)/shard_map/ppermute | solution.py:23
  77.0 72.8 %collective-permute-start.4 = (f32[4,45,64]{2,1,0:T(8,128)S(1)}, f32[4,45,64]{2,1,0:T(8,128)}, u32[]{:S(2)}, u32[]{:S(2)}) collective-permute-start(f32[4,45,64]{2,1,0:T(8,128)S(1)} %get-tuple-element.638), channel_id=1, source_target_pairs={{0,1},{1,2},{2,3},{3,4},{4,5},{5,6},{6,7},{7,8},{8,9},{9,10},{10,1... | collective-permute-start | bytes 138248 | tf_op jit(solution)/shard_map/ppermute | solution.py:22
  144.9 14.1 %all-to-all-start.2 = ((f32[90,16,32]{0,2,1:T(8,128)}), f32[90,16,32]{0,2,1:T(8,128)S(1)}, u32[]{:S(2)}, u32[]{:S(2)}) async-start(f32[90,16,32]{0,2,1:T(8,128)} %bitcast.107), calls=%async_computation.2 | async-start | bytes 524288 | tf_op jit(solution)/shard_map/all_to_all | solution.py:172
  153.4 11.9 %collective-permute-start.7 = (f32[4,45,64]{2,1,0:T(8,128)S(1)}, f32[4,45,64]{2,1,0:T(8,128)S(1)}, u32[]{:S(2)}, u32[]{:S(2)}) collective-permute-start(f32[4,45,64]{2,1,0:T(8,128)S(1)} %get-tuple-element.637), channel_id=1, source_target_pairs={{1,0},{2,1},{3,2},{4,3},{5,4},{6,5},{7,6},{8,7},{9,8},{10,9},{11,1... | collective-permute-start | bytes 138248 | tf_op jit(solution)/shard_map/ppermute | solution.py:23
  159.0 8.2 %collective-permute-start.6 = (f32[4,45,64]{2,1,0:T(8,128)S(1)}, f32[4,45,64]{2,1,0:T(8,128)S(1)}, u32[]{:S(2)}, u32[]{:S(2)}) collective-permute-start(f32[4,45,64]{2,1,0:T(8,128)S(1)} %get-tuple-element.636), channel_id=1, source_target_pairs={{0,1},{1,2},{2,3},{3,4},{4,5},{5,6},{6,7},{7,8},{8,9},{9,10},{10,1... | collective-permute-start | bytes 138248 | tf_op jit(solution)/shard_map/ppermute | solution.py:22
  162.8 7.7 %collective-permute-start.8 = (f32[3,512]{1,0:T(4,128)S(1)}, f32[3,512]{1,0:T(4,128)S(1)}, u32[]{:S(2)}, u32[]{:S(2)}) collective-permute-start(f32[3,512]{1,0:T(4,128)S(1)} %slice.1427), channel_id=1, source_target_pairs={{0,16},{1,17},{2,18},{3,19},{4,20},{5,21},{6,22},{7,23},{8,24},{9,... | collective-permute-start | bytes 18440
  (19 other events, 123.9 us)
Sparse Core Ops, SparseCore 0:
  59.7 7.9 all-gather.1
where the time goes:
time: 179 us; the launch traced here: 178 us
  starting transfers between devices  38.7 us (22%)
  local copies, waits for them, and re-layouts  33.6 us (19%)
  other arithmetic  30.1 us (17%)
  waiting for transfers between devices  22.5 us (13%)
  matrix products  18.8 us (11%)
  loops' own time  15.9 us (9%)
  between operations  15.6 us (9%)
  blocking collectives  3.04 us (2%)
    ppermute x4, starting transfers between devices, padded(): after = lax.ppermute(first, axis, down)  13.7 us
    dynamic_slice x20, local copies, waits for them, and re-layouts, compute_flux_heating(): lax.scan(down_block, down_init, block_ids)  12.4 us
    all_to_all x1, waiting for transfers between devices, per_device(): lax.all_to_all(packed, 'grp', split_axis=2, concat_axis=2, tiled=True)  12.4 us
    reduce_sum x90, other arithmetic, up_block(): upward_rows.append(jnp.sum(upward, axis=0))  11.3 us
    dot_general x4, matrix products, per_device(): jnp.dot(extended.reshape(-1, extended_span), blend_matrix, precision=TOP)  11.2 us
    all_to_all x1, starting transfers between devices, per_device(): lax.all_to_all(packed_surface, 'grp', split_axis=2, concat_axis=2, tiled=...  8.31 us
    another operation x1, loops' own time, compute_flux_heating(): lax.scan(down_block, down_init, block_ids)  8.24 us
    unnamed x85, local copies, waits for them, and re-layouts  8.12 us
  transfers between devices with their start and end apart: 13, of which 4 were waited for; matrix products, arithmetic and copies ran while one was open for 46% of the time, Pallas kernels for 0%

commit v1 on v0

--- a/solution.py
+++ b/solution.py
@@ -1,6 +1,10 @@
+import functools
+
 import jax
 import jax.numpy as jnp
 from jax import lax
+from jax.experimental import pallas as pl
+from jax.experimental.pallas import tpu as pltpu
 from jax.sharding import PartitionSpec as P
 
 STEPS = 4
@@ -108,7 +112,7 @@
     return (net_flux[:-1] - net_flux[1:]) / radiant_depth
 
 
-def per_device(
+def plain_device(
     stratum_warmth_anomaly,
     pressure_depth,
     absorber_amounts,
@@ -194,6 +198,390 @@
     return (heating, mixed)
 
 
+LANES = 128
+NT = (((1,), (1,)), ((), ()))
+VMEM = pl.BlockSpec(memory_space=pltpu.VMEM)
+MESH = pl.DeviceIdType.MESH
+
+
+def halves(value):
+    high = value.astype(jnp.bfloat16)
+    low = (value - high.astype(jnp.float32)).astype(jnp.bfloat16)
+    return high, low
+
+
+def iota(shape, dim):
+    return lax.broadcasted_iota(jnp.int32, shape, dim)
+
+
+def one_hot(cond):
+    return jnp.where(cond, 1.0, 0.0).astype(jnp.bfloat16)
+
+
+def mm(left, right, dims=(((1,), (0,)), ((), ()))):
+    return lax.dot_general(left, right, dims, preferred_element_type=jnp.float32)
+
+
+def greet(n):
+    me, side = lax.axis_index("grp"), lax.axis_index("sec")
+    barrier = pltpu.get_barrier_semaphore()
+    for d in range(1, n):
+        peer = lax.rem(me + d, n)
+        pl.semaphore_signal(barrier, inc=1, device_id={"grp": peer}, device_id_type=MESH)
+    pl.semaphore_signal(barrier, inc=1, device_id={"sec": 1 - side}, device_id_type=MESH)
+    pl.semaphore_wait(barrier, n)
+    return me, side
+
+
+def remote(src, dst, send_sem, recv_sem, device):
+    return pltpu.make_async_remote_copy(
+        src_ref=src, dst_ref=dst, send_sem=send_sem, recv_sem=recv_sem,
+        device_id=device, device_id_type=MESH,
+    )
+
+
+def dispatch_kernel(
+    n, temp, depth, absorb, ground, sun, mask, pos, memb, adj, blend,
+    mixed_out, pooled_out,
+    data, send, recv, halo_l, halo_r, adj_l, adj_r, blend_l, blend_r,
+    grid_a, grid_b, mix_hi, mix_lo, pooled,
+    out_sem, in_sem, hs_sem, hr_sem, ps_sem, pr_sem,
+):
+    species, levels, cols = absorb.shape
+    rows = -(-(levels + 3) // 8) * 8
+    per = cols // n
+    pack = per // 4
+    rads = cols // 4
+    wide = STEPS * HALO
+    me, side = greet(n)
+    right, left = lax.rem(me + 1, n), lax.rem(me + n - 1, n)
+
+    halo = []
+    for k, (src, to_left, to_right) in enumerate(
+        ((absorb, halo_r, halo_l), (adj, adj_r, adj_l), (blend, blend_r, blend_l))
+    ):
+        lead = (slice(None),) * (len(src.shape) - 1)
+        first, last = src.at[lead + (pl.ds(0, wide),)], src.at[lead + (pl.ds(cols - wide, wide),)]
+        halo.append(remote(first, to_left, hs_sem.at[2 * k], hr_sem.at[2 * k], {"grp": left}))
+        halo.append(remote(last, to_right, hs_sem.at[2 * k + 1], hr_sem.at[2 * k + 1], {"grp": right}))
+    for copy in halo:
+        copy.start()
+
+    data[...] = jnp.zeros_like(data)
+    data[0:levels, :] = temp[...]
+    data[rows : rows + levels, :] = depth[...]
+    for s in range(species):
+        data[(2 + s) * rows : (2 + s) * rows + levels, :] = absorb[s]
+    data[levels : levels + 1, :] = ground[...]
+    data[levels + 1 : levels + 2, :] = sun[...]
+    data[levels + 2 : levels + 3, :] = mask[...].astype(jnp.float32) * sun[...]
+    rest = data[2 * LANES : 2 * LANES + 32, :]
+    for q in range(1, 4):
+        data[2 * LANES + 32 * q : 2 * LANES + 32 * (q + 1), :] = rest
+    data_hi, data_lo = halves(data[...])
+    relative = pos[...] - me * per
+    relative = jnp.where(relative < 0, relative + cols, relative)
+    chunk = 4 * per
+    lane_block = iota((4, pack, LANES), 2) // 32
+    copies = []
+    for c in range(n // 4):
+        hot = one_hot(iota((chunk, cols), 0) + c * chunk == relative)
+        out = mm(hot, data_hi, NT) + mm(hot, data_lo, NT)
+        send[4 * c : 4 * c + 4, 0:per, :] = out[:, 0:LANES].reshape(4, per, LANES)
+        send[4 * c : 4 * c + 4, per : 2 * per, :] = out[:, LANES : 2 * LANES].reshape(4, per, LANES)
+        tail = out[:, 2 * LANES :].reshape(4, 4, pack, LANES)
+        folded = jnp.where(lane_block == 0, tail[:, 0], 0.0)
+        for q in range(1, 4):
+            folded = jnp.where(lane_block == q, tail[:, q], folded)
+        send[4 * c : 4 * c + 4, 2 * per :, :] = folded
+        for d in range(max(4 * c, 1), 4 * c + 4):
+            copy = remote(
+                send.at[d], recv.at[me], out_sem.at[d], in_sem.at[d], {"grp": lax.rem(me + d, n)}
+            )
+            copy.start()
+            copies.append(copy)
+    recv[me] = send[0]
+
+    grid_a[...] = jnp.zeros_like(grid_a)
+    grid_b[...] = jnp.zeros_like(grid_b)
+    for s in range(species):
+        grid_a[s * rows : s * rows + levels, wide : wide + cols] = absorb[s]
+    for copy in halo:
+        copy.wait()
+    for s in range(species):
+        grid_a[s * rows : s * rows + levels, 0:wide] = halo_l[s]
+        grid_a[s * rows : s * rows + levels, wide + cols :] = halo_r[s]
+    span = cols + 2 * wide
+    tables = (
+        (adj_l[...] - HALO + wide - cols, blend_l[...]),
+        (adj[...] - HALO + wide, blend[...]),
+        (adj_r[...] - HALO + wide + cols, blend_r[...]),
+    )
+    table = jnp.concatenate([t[0] for t in tables], axis=1)
+    weight = jnp.concatenate([t[1] for t in tables], axis=1)
+    total = jnp.sum(weight, axis=0, keepdims=True)
+    width = 256
+    windows = []
+    for b in range(span // width):
+        low, high = max(0, width * b - LANES), min(span, width * (b + 1) + LANES)
+        windows.append((low, high))
+        source = iota((high - low, width), 0) + low
+        matrix = jnp.zeros((high - low, width), jnp.float32)
+        here = slice(width * b, width * (b + 1))
+        for k in range(table.shape[0]):
+            matrix = matrix + jnp.where(table[k : k + 1, here] == source, weight[k : k + 1, here], 0.0)
+        hi, lo = halves(matrix)
+        mix_hi[b, 0 : high - low, :] = hi
+        mix_lo[b, 0 : high - low, :] = lo
+    old, new = grid_a, grid_b
+    for step in range(STEPS):
+        blocks = range(span // width)
+        if step == STEPS - 1:
+            blocks = range(wide // width, (wide + cols) // width)
+        for b in blocks:
+            low, high = windows[b]
+            here = slice(width * b, width * (b + 1))
+            hi, lo = halves(old[:, low:high])
+            left_hi = mix_hi[b, 0 : high - low, :]
+            update = mm(hi, left_hi) + mm(lo, left_hi) + mm(hi, mix_lo[b, 0 : high - low, :])
+            centre = old[:, here]
+            new[:, here] = centre + (update - total[:, here] * centre)
+        old, new = new, old
+    for s in range(species):
+        mixed_out[s] = old[s * rows : s * rows + levels, wide : wide + cols]
+
+    member = one_hot(iota((rads, cols), 0) == lax.shift_right_logical(memb[...], 2))
+    for copy in copies:
+        copy.wait()
+    whole = recv[...]
+    parts = [whole[:, 0:per, :].reshape(cols, LANES), whole[:, per : 2 * per, :].reshape(cols, LANES)]
+    tail = whole[:, 2 * per :, :]
+    big_block = iota((n, pack, LANES), 2) // 32
+    tail = jnp.stack([jnp.where(big_block == q, tail, 0.0) for q in range(4)], axis=1)
+    parts.append(tail.reshape(cols, LANES))
+    for k, part in enumerate(parts):
+        hi, lo = halves(part)
+        pooled[side, k] = (mm(member, hi) + mm(member, lo)) * 0.25
+    copy = remote(pooled.at[side], pooled.at[side], ps_sem, pr_sem, {"sec": 1 - side})
+    copy.start()
+    copy.wait()
+    pooled_out[...] = pooled[...]
+
+
+def dispatch(n, *args):
+    absorb = args[2]
+    species, levels, cols = absorb.shape
+    rows = -(-(levels + 3) // 8) * 8
+    per = cols // n
+    slab = 2 * per + per // 4
+    wide = STEPS * HALO
+    near = args[8].shape[0]
+    span = cols + 2 * wide
+    dma = pltpu.SemaphoreType.DMA
+    f32 = jnp.float32
+    return pl.pallas_call(
+        functools.partial(dispatch_kernel, n),
+        out_shape=(
+            jax.ShapeDtypeStruct(absorb.shape, f32),
+            jax.ShapeDtypeStruct((2, 3, cols // 4, LANES), f32),
+        ),
+        in_specs=[VMEM] * len(args),
+        out_specs=(VMEM, VMEM),
+        scratch_shapes=[
+            pltpu.VMEM((3 * LANES, cols), f32),
+            pltpu.VMEM((n, slab, LANES), f32),
+            pltpu.VMEM((n, slab, LANES), f32),
+            pltpu.VMEM((species, levels, wide), f32),
+            pltpu.VMEM((species, levels, wide), f32),
+            pltpu.VMEM((near, wide), jnp.int32),
+            pltpu.VMEM((near, wide), jnp.int32),
+            pltpu.VMEM((near, wide), f32),
+            pltpu.VMEM((near, wide), f32),
+            pltpu.VMEM((species * rows, span), f32),
+            pltpu.VMEM((species * rows, span), f32),
+            pltpu.VMEM((span // 256, 512, 256), jnp.bfloat16),
+            pltpu.VMEM((span // 256, 512, 256), jnp.bfloat16),
+            pltpu.VMEM((2, 3, cols // 4, LANES), f32),
+            dma((n,)), dma((n,)), dma((6,)), dma((6,)), dma, dma,
+        ],
+        compiler_params=pltpu.CompilerParams(
+            collective_id=0, has_side_effects=True, vmem_limit_bytes=40 << 20
+        ),
+        cost_estimate=pl.CostEstimate(flops=10**9, bytes_accessed=4 << 20, transcendentals=0),
+    )(*args)
+
+
+def sweep_kernel(n, levels, pooled, memb, opacity, emission, sunshine, slots_out, state, trans, net):
+    rows = -(-(levels + 3) // 8) * 8
+    gpoints = emission.shape[0]
+    strata = opacity.shape[2]
+    rads = pooled.shape[2]
+    cols = memb.shape[1]
+    for h in range(2):
+        state[h, 0:LANES, :] = pooled[h, 0].T
+        state[h, LANES : 2 * LANES, :] = pooled[h, 1].T
+        tail = pooled[h, 2].T
+        state[h, 2 * LANES :, :] = tail[0:32] + tail[32:64] + tail[64:96] + tail[96:128]
+
+    def row(field, level):
+        at = field * rows + level % levels
+        return state[level // levels, at : at + 1, :]
+
+    ground = state[0, levels : levels + 1, :]
+    incline = state[0, levels + 1 : levels + 2, :]
+    incoming = state[0, levels + 2 : levels + 3, :]
+    share = jnp.broadcast_to(emission[...], (gpoints, rads))
+    slant = -1.0 / incline
+
+    def gsum(value):
+        return jnp.sum(value.reshape(gpoints // 8, 8, rads), axis=0)
+
+    def fourth(value):
+        square = value * value
+        return square * square
+
+    thermal = jnp.zeros((gpoints, rads), jnp.float32)
+    direct = sunshine[...] * incoming
+    net[0] = gsum(direct)
+    for level in range(strata):
+        tau = opacity[0, :, level : level + 1] * row(2, level)
+        for s in range(1, opacity.shape[0]):
+            tau = tau + opacity[s, :, level : level + 1] * row(2 + s, level)
+        transmit = jnp.exp(-DIFFUSE * tau)
+        trans[level] = transmit
+        source = share * fourth(row(0, level))
+        thermal = source + transmit * (thermal - source)
+        direct = direct * jnp.exp(tau * slant)
+        net[level + 1] = gsum(thermal + direct)
+    upward = share * fourth(ground)
+    net[strata] = net[strata] - gsum(upward)
+    for level in range(strata - 1, -1, -1):
+        source = share * fourth(row(0, level))
+        upward = source + trans[level] * (upward - source)
+        net[level] = net[level] - gsum(upward)
+
+    member = one_hot(iota((rads, cols), 0) == lax.shift_right_logical(memb[...], 2))
+    per = cols // n
+    fold = per // 2
+    half_lane = iota((n, fold, LANES), 2) // 64
+    fill = jnp.zeros((64 - levels, rads), jnp.float32)
+    for h in range(2):
+        change = net[h * levels : (h + 1) * levels] - net[h * levels + 1 : (h + 1) * levels + 1]
+        heat = jnp.sum(change, axis=1) / state[h, rows : rows + levels, :]
+        heat = jnp.concatenate([heat, fill], axis=0)
+        hi, lo = halves(jnp.concatenate([heat, heat], axis=0))
+        spread = (mm(hi, member) + mm(lo, member)).T.reshape(n, 2, fold, LANES)
+        slots_out[h] = jnp.where(half_lane == 0, spread[:, 0], spread[:, 1])
+
+
+def sweep(n, levels, pooled, memb, opacity, emission, sunshine):
+    rows = -(-(levels + 3) // 8) * 8
+    gpoints = emission.shape[0]
+    strata = opacity.shape[2]
+    rads = pooled.shape[2]
+    per = memb.shape[1] // n
+    f32 = jnp.float32
+    return pl.pallas_call(
+        functools.partial(sweep_kernel, n, levels),
+        out_shape=jax.ShapeDtypeStruct((2, n, per // 2, LANES), f32),
+        in_specs=[VMEM] * 5,
+        out_specs=VMEM,
+        scratch_shapes=[
+            pltpu.VMEM((2, 6 * rows, rads), f32),
+            pltpu.VMEM((strata, gpoints, rads), f32),
+            pltpu.VMEM((strata + 1, 8, rads), f32),
+        ],
+        compiler_params=pltpu.CompilerParams(vmem_limit_bytes=40 << 20),
+        cost_estimate=pl.CostEstimate(flops=2 * 10**7, bytes_accessed=1 << 20, transcendentals=10**6),
+    )(pooled, memb, opacity, emission, sunshine)
+
+
+def return_kernel(n, slots, out, other, send, recv, s_sem, r_sem, out_sem, in_sem):
+    me, side = greet(n)
+    copy = remote(slots.at[1 - side], other, s_sem, r_sem, {"sec": 1 - side})
+    copy.start()
+    copy.wait()
+    send[...] = slots[side] + other[...]
+    copies = []
+    for d in range(1, n):
+        peer = lax.rem(me + d, n)
+        copy = remote(send.at[peer], recv.at[me], out_sem.at[d], in_sem.at[d], {"grp": peer})
+        copy.start()
+        copies.append(copy)
+    recv[me] = send[me]
+    for copy in copies:
+        copy.wait()
+    out[...] = recv[...]
+
+
+def give_back(n, slots):
+    shape = slots.shape[1:]
+    f32 = jnp.float32
+    dma = pltpu.SemaphoreType.DMA
+    return pl.pallas_call(
+        functools.partial(return_kernel, n),
+        out_shape=jax.ShapeDtypeStruct(shape, f32),
+        in_specs=[VMEM],
+        out_specs=VMEM,
+        scratch_shapes=[
+            pltpu.VMEM(shape, f32), pltpu.VMEM(shape, f32), pltpu.VMEM(shape, f32),
+            dma, dma, dma((n,)), dma((n,)),
+        ],
+        compiler_params=pltpu.CompilerParams(collective_id=1, has_side_effects=True),
+        cost_estimate=pl.CostEstimate(flops=10**5, bytes_accessed=1 << 20, transcendentals=0),
+    )(slots)
+
+
+def unpack_kernel(n, returned, pos, heating):
+    levels, cols = heating.shape
+    fold = returned.shape[1]
+    value = returned[...].reshape(n * fold, LANES).T
+    place = iota((n * fold, cols), 0)
+    place = (place // fold) * (2 * fold) + lax.rem(place, fold)
+    total = None
+    for q in range(2):
+        hot = one_hot(place + q * fold == pos[...])
+        hi, lo = halves(value[64 * q : 64 * (q + 1)])
+        part = mm(hi, hot) + mm(lo, hot)
+        total = part if total is None else total + part
+    heating[...] = total[0:levels]
+
+
+def unpack(n, levels, returned, pos):
+    return pl.pallas_call(
+        functools.partial(unpack_kernel, n),
+        out_shape=jax.ShapeDtypeStruct((levels, pos.shape[1]), jnp.float32),
+        in_specs=[VMEM] * 2,
+        out_specs=VMEM,
+        compiler_params=pltpu.CompilerParams(vmem_limit_bytes=32 << 20),
+        cost_estimate=pl.CostEstimate(flops=10**8, bytes_accessed=1 << 20, transcendentals=0),
+    )(returned, pos)
+
+
+def folds_evenly(n, sides, levels, cols, species, gpoints):
+    rows = -(-(levels + 3) // 8) * 8
+    return (
+        n > 3 and n % 4 == 0 and sides == 2 and species == 4
+        and cols == n * 32 and cols == 4 * LANES and 2 * STEPS * HALO == cols
+        and 6 * rows == 2 * LANES + 32 and gpoints % 8 == 0
+    )
+
+
+def per_device(*args):
+    (warmth, depth, absorb, ground, sun, mask, pos, memb, adj, blend, opacity, emission, sunshine) = args
+    n = lax.axis_size("grp")
+    levels, cols = warmth.shape
+    gpoints = emission.shape[0]
+    if not folds_evenly(n, lax.axis_size("sec"), levels, cols, absorb.shape[0], gpoints):
+        return plain_device(*args)
+    mixed, pooled = dispatch(
+        n, warmth, depth, absorb, ground[None], sun[None], mask[None], pos, memb, adj, blend
+    )
+    slots = sweep(n, levels, pooled, memb, opacity, emission[:, None], sunshine[:, None])
+    returned = give_back(n, slots)
+    return (unpack(n, levels, returned, pos), mixed)
+
+
 def solution(mesh):
     in_specs = (
         P("sec", "grp"),

time: 179 us -> 51.2 us (0.29)
  Pallas kernels: 0 us -> 44.3 us
  starting transfers between devices: 38.7 us -> 0 us
  other arithmetic: 30.1 us -> 0 us
  local copies, waits for them, and re-layouts: 33.6 us -> 5.92 us
  waiting for transfers between devices: 22.5 us -> 0 us
  matrix products: 18.8 us -> 0 us
  loops' own time: 15.9 us -> 0 us
  between operations: 15.6 us -> 0.82 us
  blocking collectives: 3.04 us -> 0 us
    pallas_call x0 -> x4, Pallas kernels: none -> 44.3 us  [the longest x1 28.6 us: dispatch(): pl.pallas_call(functools.partial(dispatch_kernel, n), out_shape=(jax.Shap...]
    reduce_sum x271 -> x0, other arithmetic: 26.5 us -> none  [the longest x90 11.3 us: up_block(): upward_rows.append(jnp.sum(upward, axis=0))]
    all_to_all x3 -> x0, starting transfers between devices: 20.4 us -> none  [the longest x1 8.31 us: per_device(): lax.all_to_all(packed_surface, 'grp', split_axis=2, concat_axis=2, tiled=...]
    dot_general x10 -> x0, matrix products: 18.8 us -> none  [the longest x4 11.2 us: per_device(): jnp.dot(extended.reshape(-1, extended_span), blend_matrix, precision=TOP)]
    another operation x2 -> x0, loops' own time: 15.9 us -> none  [the longest x1 8.24 us: compute_flux_heating(): lax.scan(down_block, down_init, block_ids)]
    ppermute x8 -> x0, starting transfers between devices: 15.8 us -> none  [the longest x4 13.7 us: padded(): after = lax.ppermute(first, axis, down)]
    dynamic_slice x40 -> x0, local copies, waits for them, and re-layouts: 12.9 us -> none  [the longest x20 12.4 us: compute_flux_heating(): lax.scan(down_block, down_init, block_ids)]
    all_to_all x3 -> x0, waiting for transfers between devices: 12.4 us -> none  [the longest x1 12.4 us: per_device(): lax.all_to_all(packed, 'grp', split_axis=2, concat_axis=2, tiled=True)]
  transfers between devices with their start and end apart: 13 -> 0, of which waited for: 4 -> 0; matrix products, arithmetic and copies ran while one was open for 46% -> 0% of each run, Pallas kernels for 0% -> 0%
where the time goes in v1:
time: 51.2 us; the launch traced here: 51 us
  Pallas kernels  44.3 us (87%)
  local copies, waits for them, and re-layouts  5.92 us (12%)
  between operations  0.82 us (2%)
    pallas_call x1, Pallas kernels, dispatch(): pl.pallas_call(functools.partial(dispatch_kernel, n), out_shape=(jax.Shap...  28.6 us
    pallas_call x1, Pallas kernels, give_back(): pl.pallas_call(functools.partial(return_kernel, n), out_shape=jax.ShapeDt...  10.6 us
    unnamed x30, local copies, waits for them, and re-layouts  5.73 us
    pallas_call x1, Pallas kernels, sweep(): pl.pallas_call(functools.partial(sweep_kernel, n, levels), out_shape=jax....  4.05 us

profile of v1, /device:TPU:0, one launch (start us, length us, event | category | flops | bytes accessed | tf_op | source)
XLA Modules:
  0.0 51.0 jit_solution(15629976672474969612)
XLA Ops:
  0.6 0.0 copy-start.3
  0.6 0.0 copy-start.4
  0.7 0.0 copy-start.5
  0.7 0.0 copy-start.6
  0.7 0.0 copy-start.8
  0.7 0.0 copy-start.9
  0.7 0.0 copy-start.10
  0.7 0.0 copy-start.11
  0.7 1.2 %copy.15.absorb = f32[4,45,512]{2,1,0:T(8,128)S(1)} copy(f32[4,45,512]{2,0,1:T(4,128)} %param.15) | data formatting | bytes 737280 | tf_op args[2]
  1.9 0.0 copy-start.7
  1.9 0.0 copy-done.3
  2.0 0.0 copy-done.4
  2.0 0.0 copy-done.5
  2.0 0.0 copy-done.6
  2.0 0.0 copy-done.8
  2.0 0.0 copy-done.9
  2.0 0.0 copy-done.10
  2.0 0.0 copy-done.11
  2.0 0.6 %copy-done.7 = f32[512]{0:T(512)S(1)} copy-done((f32[512]{0:T(512)S(1)}, f32[512]{0:T(512)}, u32[]{:S(2)}) %copy-start.7) | copy-done | bytes 2072
  2.6 28.6 %shard_map.140 = (f32[4,45,512]{2,1,0:T(8,128)S(1)}, f32[2,3,128,128]{3,2,1,0:T(8,128)S(1)}) custom-call(f32[45,512]{1,0:T(8,128)S(1)} %copy-done.3, f32[45,512]{1,0:T(8,128)S(1)} %copy-done.4, f32[4,45,512]{2,1,0:T(8,128)S(1)} %copy.15.absorb, f32[1,512]{1,0:T(1,128)S(1)} %bitcast.5, f32[1,512]{1,0:T(1,128)S(1)} %bitcast.6, s32[1,512]{1,0:T(1,128)S(1)} %bitcast.7, ...), custom_call_target="tpu_custom_call" | custom-call | flops 1000000000 | bytes 4194304 | tf_op jit(solution)/shard_map/pallas_call | solution.py:382
  31.2 0.0 copy-start.12
  31.3 0.6 %copy-done.12 = f32[56]{0:T(128)S(1)} copy-done((f32[56]{0:T(128)S(1)}, f32[56]{0:T(128)}, u32[]{:S(2)}) %copy-start.12) | copy-done | bytes 248
  31.9 0.1 copy.16.emission
  32.0 0.7 %copy-done.13 = f32[56]{0:T(128)S(1)} copy-done((f32[56]{0:T(128)S(1)}, f32[56]{0:T(128)}, u32[]{:S(2)}) %copy-start.13) | copy-done | bytes 248
  32.6 0.1 copy.17.sunshine
  32.7 4.0 %shard_map.141.slots = f32[2,16,16,128]{3,2,1,0:T(8,128)S(1)} custom-call(f32[2,3,128,128]{3,2,1,0:T(8,128)S(1)} %get-tuple-element.4.pooled, s32[1,512]{1,0:T(1,128)S(1)} %copy-done.10, f32[4,56,90]{2,1,0:T(8,128)S(1)} %copy-done.2, f32[56,1]{1,0:T(8,128)S(1)} %copy.16.emission, f32[56,1]{1,0:T(8,128)S(1)} %copy.17.sunshine), custom_call_target="tpu_custom_call" | custom-call | flops 20000000 | bytes 1048576 | tf_op jit(solution)/shard_map/pallas_call | solution.py:484
  36.8 0.0 copy-start
  36.8 0.7 %copy-done = f32[2,16,16,128]{3,2,1,0:T(8,128)} copy-done((f32[2,16,16,128]{3,2,1,0:T(8,128)}, f32[2,16,16,128]{3,2,1,0:T(8,128)S(1)}, u32[]{:S(2)}) %copy-start) | copy-done | bytes 262168
  37.5 10.6 %shard_map.142.returned = f32[16,16,128]{2,1,0:T(8,128)} custom-call(f32[2,16,16,128]{3,2,1,0:T(8,128)} %copy-done), custom_call_target="tpu_custom_call" | custom-call | flops 100000 | bytes 1048576 | tf_op jit(solution)/shard_map/pallas_call | solution.py:521
  48.1 0.9 %copy-done.1 = f32[16,16,128]{2,1,0:T(8,128)S(1)} copy-done((f32[16,16,128]{2,1,0:T(8,128)S(1)}, f32[16,16,128]{2,1,0:T(8,128)}, u32[]{:S(2)}) %copy-start.1) | copy-done | bytes 131096
  49.0 1.0 %shard_map.143 = f32[45,512]{1,0:T(8,128)} custom-call(f32[16,16,128]{2,1,0:T(8,128)S(1)} %copy-done.1, s32[1,512]{1,0:T(1,128)S(1)} %copy-done.11), custom_call_target="tpu_custom_call" | custom-call | flops 100000000 | bytes 1048576 | tf_op jit(solution)/shard_map/pallas_call | solution.py:551
  50.0 1.0 %copy.18 = f32[4,45,512]{2,0,1:T(4,128)} copy(f32[4,45,512]{2,1,0:T(8,128)S(1)} %get-tuple-element.7) | data formatting | bytes 737280
  (4 shorter events, 0.0 us)
Async XLA Ops:
  0.6 1.3 %copy-start.3 = (f32[45,512]{1,0:T(8,128)S(1)}, f32[45,512]{1,0:T(8,128)}, u32[]{:S(2)}) copy-start(f32[45,512]{1,0:T(8,128)} %temp.1) | copy-start | bytes 276484
  0.6 1.3 %copy-start.4 = (f32[45,512]{1,0:T(8,128)S(1)}, f32[45,512]{1,0:T(8,128)}, u32[]{:S(2)}) copy-start(f32[45,512]{1,0:T(8,128)} %depth.1) | copy-start | bytes 276484
  0.7 1.3 %copy-start.5 = (s32[6,512]{1,0:T(8,128)S(1)}, s32[6,512]{1,0:T(8,128)}, u32[]{:S(2)}) copy-start(s32[6,512]{1,0:T(8,128)} %adj.1) | copy-start | bytes 36868
  0.7 1.3 %copy-start.6 = (f32[6,512]{1,0:T(8,128)S(1)}, f32[6,512]{1,0:T(8,128)}, u32[]{:S(2)}) copy-start(f32[6,512]{1,0:T(8,128)} %blend.1) | copy-start | bytes 36868
  0.7 1.3 %copy-start.8 = (f32[512]{0:T(512)S(1)}, f32[512]{0:T(512)}, u32[]{:S(2)}) copy-start(f32[512]{0:T(512)} %param.17) | copy-start | bytes 6148
  0.7 1.3 %copy-start.9 = (s32[512]{0:T(512)S(1)}, s32[512]{0:T(512)}, u32[]{:S(2)}) copy-start(s32[512]{0:T(512)} %param.18) | copy-start | bytes 6148
  0.7 1.3 %copy-start.10 = (s32[1,512]{1,0:T(1,128)S(1)}, s32[1,512]{1,0:T(1,128)}, u32[]{:S(2)}) copy-start(s32[1,512]{1,0:T(1,128)} %memb.3) | copy-start | bytes 6148
  0.7 1.3 %copy-start.11 = (s32[1,512]{1,0:T(1,128)S(1)}, s32[1,512]{1,0:T(1,128)}, u32[]{:S(2)}) copy-start(s32[1,512]{1,0:T(1,128)} %pos.3) | copy-start | bytes 6148
  1.9 0.7 %copy-start.7 = (f32[512]{0:T(512)S(1)}, f32[512]{0:T(512)}, u32[]{:S(2)}) copy-start(f32[512]{0:T(512)} %param.16) | copy-start | bytes 6148
  2.6 30.1 %copy-start.2 = (f32[4,56,90]{2,1,0:T(8,128)S(1)}, f32[4,56,90]{2,1,0:T(8,128)}, u32[]{:S(2)}) copy-start(f32[4,56,90]{2,1,0:T(8,128)} %opacity.1) | copy-start | bytes 241924
  31.2 0.7 %copy-start.12 = (f32[56]{0:T(128)S(1)}, f32[56]{0:T(128)}, u32[]{:S(2)}) copy-start(f32[56]{0:T(128)} %param.24) | copy-start | bytes 676
  32.0 0.7 %copy-start.13 = (f32[56]{0:T(128)S(1)}, f32[56]{0:T(128)}, u32[]{:S(2)}) copy-start(f32[56]{0:T(128)} %param.25) | copy-start | bytes 676
  36.8 0.7 %copy-start = (f32[2,16,16,128]{3,2,1,0:T(8,128)}, f32[2,16,16,128]{3,2,1,0:T(8,128)S(1)}, u32[]{:S(2)}) copy-start(f32[2,16,16,128]{3,2,1,0:T(8,128)S(1)} %shard_map.141.slots) | copy-start | bytes 786436
  48.1 0.9 %copy-start.1 = (f32[16,16,128]{2,1,0:T(8,128)S(1)}, f32[16,16,128]{2,1,0:T(8,128)}, u32[]{:S(2)}) copy-start(f32[16,16,128]{2,1,0:T(8,128)} %shard_map.142.returned) | copy-start | bytes 393220

commit v2 on v1

--- a/solution.py
+++ b/solution.py
@@ -240,12 +240,13 @@
     )
 
 
-def dispatch_kernel(
+def device_kernel(
     n, temp, depth, absorb, ground, sun, mask, pos, memb, adj, blend,
-    mixed_out, pooled_out,
+    opacity, emission, sunshine, heating, mixed_out,
     data, send, recv, halo_l, halo_r, adj_l, adj_r, blend_l, blend_r,
     grid_a, grid_b, mix_hi, mix_lo, pooled,
-    out_sem, in_sem, hs_sem, hr_sem, ps_sem, pr_sem,
+    state, opac, trans, net, heat, other, back, home,
+    out_sem, in_sem, hs_sem, hr_sem, ps_sem, pr_sem, ts_sem, tr_sem, bo_sem, bi_sem,
 ):
     species, levels, cols = absorb.shape
     rows = -(-(levels + 3) // 8) * 8
@@ -350,7 +351,19 @@
     for s in range(species):
         mixed_out[s] = old[s * rows : s * rows + levels, wide : wide + cols]
 
+    gpoints = emission.shape[1]
+    strata = opacity.shape[2]
+    for b in range(strata // LEVEL_BLOCK):
+        for k in range(species):
+            opac[b, k * gpoints : (k + 1) * gpoints, 0:LEVEL_BLOCK] = opacity[
+                k, :, b * LEVEL_BLOCK : (b + 1) * LEVEL_BLOCK
+            ]
+    diagonal = iota((gpoints, gpoints), 0) == iota((gpoints, gpoints), 1)
+    share = jnp.sum(jnp.where(diagonal, emission[...], 0.0), axis=1, keepdims=True)
+    sunny = jnp.sum(jnp.where(diagonal, sunshine[...], 0.0), axis=1, keepdims=True)
+    share = jnp.broadcast_to(share, (gpoints, rads))
     member = one_hot(iota((rads, cols), 0) == lax.shift_right_logical(memb[...], 2))
+
     for copy in copies:
         copy.wait()
     whole = recv[...]
@@ -365,10 +378,92 @@
     copy = remote(pooled.at[side], pooled.at[side], ps_sem, pr_sem, {"sec": 1 - side})
     copy.start()
     copy.wait()
-    pooled_out[...] = pooled[...]
-
-
-def dispatch(n, *args):
+
+    for h in range(2):
+        tail = pooled[h, 2].T
+        tail = tail[0:32] + tail[32:64] + tail[64:96] + tail[96:128]
+        field = jnp.concatenate([pooled[h, 0].T, pooled[h, 1].T, tail], axis=0)
+        for k in range(2 + species):
+            state[k, h * levels : (h + 1) * levels, :] = field[k * rows : k * rows + levels]
+        surface = field[levels : levels + 3]
+
+    def fourth(value):
+        square = value * value
+        return square * square
+
+    def gsum(value):
+        return jnp.sum(value.reshape(gpoints // 8, 8, rads), axis=0)
+
+    slant = -1.0 / surface[1:2]
+    state[0, 0:strata, :] = fourth(state[0, 0:strata, :])
+
+    def down(b, fluxes):
+        thermal, direct = fluxes
+        coeffs = opac[b]
+        for i in range(LEVEL_BLOCK):
+            level = b * LEVEL_BLOCK + i
+            tau = None
+            for k in range(species):
+                part = coeffs[k * gpoints : (k + 1) * gpoints, i : i + 1] * state[2 + k, pl.ds(level, 1), :]
+                tau = part if tau is None else tau + part
+            transmit = jnp.exp(-DIFFUSE * tau)
+            trans[level] = transmit
+            source = share * state[0, pl.ds(level, 1), :]
+            thermal = source + transmit * (thermal - source)
+            direct = direct * jnp.exp(tau * slant)
+            net[level + 1] = gsum(thermal + direct)
+        return thermal, direct
+
+    direct = sunny * surface[2:3]
+    net[0] = gsum(direct)
+    lax.fori_loop(0, strata // LEVEL_BLOCK, down, (jnp.zeros((gpoints, rads), jnp.float32), direct))
+    upward = share * fourth(surface[0:1])
+    net[strata] = net[strata] - gsum(upward)
+
+    def up(b, upward):
+        for i in range(LEVEL_BLOCK):
+            level = strata - 1 - (b * LEVEL_BLOCK + i)
+            source = share * state[0, pl.ds(level, 1), :]
+            upward = source + trans[level] * (upward - source)
+            net[level] = net[level] - gsum(upward)
+        return upward
+
+    lax.fori_loop(0, strata // LEVEL_BLOCK, up, upward)
+    heat[...] = jnp.zeros_like(heat)
+    for h in range(2):
+        change = net[h * levels : (h + 1) * levels] - net[h * levels + 1 : (h + 1) * levels + 1]
+        heat[h, 0:levels] = jnp.sum(change, axis=1) / state[1, h * levels : (h + 1) * levels, :]
+    copy = remote(heat.at[1 - side], other, ts_sem, tr_sem, {"sec": 1 - side})
+    copy.start()
+    copy.wait()
+    own = heat[side] + other[...]
+    fold = per // 2
+    hi, lo = halves(jnp.concatenate([own, own], axis=0))
+    spread = (mm(hi, member) + mm(lo, member)).T.reshape(n, 2, fold, LANES)
+    back[...] = jnp.where(iota((n, fold, LANES), 2) // 64 == 0, spread[:, 0], spread[:, 1])
+    copies = []
+    for d in range(1, n):
+        peer = lax.rem(me + d, n)
+        copy = remote(back.at[peer], home.at[me], bo_sem.at[d], bi_sem.at[d], {"grp": peer})
+        copy.start()
+        copies.append(copy)
+    home[me] = back[me]
+    place = iota((n * fold, cols), 0)
+    place = (place // fold) * (2 * fold) + lax.rem(place, fold) - pos[...]
+    hots = [one_hot(place + q * fold == 0) for q in range(2)]
+    for copy in copies:
+        copy.wait()
+    value = home[...].reshape(n * fold, LANES).T
+    hi, lo = halves(value)
+    total = None
+    for q in range(2):
+        here = slice(64 * q, 64 * (q + 1))
+        part = mm(hi[here], hots[q]) + mm(lo[here], hots[q])
+        total = part if total is None else total + part
+    heating[...] = total[0:levels]
+
+
+def one_kernel(n, *args):
     absorb = args[2]
     species, levels, cols = absorb.shape
     rows = -(-(levels + 3) // 8) * 8
@@ -376,14 +471,15 @@
     slab = 2 * per + per // 4
     wide = STEPS * HALO
     near = args[8].shape[0]
+    gpoints, strata = args[10].shape[1:]
     span = cols + 2 * wide
     dma = pltpu.SemaphoreType.DMA
     f32 = jnp.float32
     return pl.pallas_call(
-        functools.partial(dispatch_kernel, n),
+        functools.partial(device_kernel, n),
         out_shape=(
+            jax.ShapeDtypeStruct((levels, cols), f32),
             jax.ShapeDtypeStruct(absorb.shape, f32),
-            jax.ShapeDtypeStruct((2, 3, cols // 4, LANES), f32),
         ),
         in_specs=[VMEM] * len(args),
         out_specs=(VMEM, VMEM),
@@ -402,160 +498,21 @@
             pltpu.VMEM((span // 256, 512, 256), jnp.bfloat16),
             pltpu.VMEM((span // 256, 512, 256), jnp.bfloat16),
             pltpu.VMEM((2, 3, cols // 4, LANES), f32),
-            dma((n,)), dma((n,)), dma((6,)), dma((6,)), dma, dma,
+            pltpu.VMEM((2 + species, -(-strata // 8) * 8, cols // 4), f32),
+            pltpu.VMEM((strata // LEVEL_BLOCK, species * gpoints, LANES), f32),
+            pltpu.VMEM((strata, gpoints, cols // 4), f32),
+            pltpu.VMEM((strata + 1, 8, cols // 4), f32),
+            pltpu.VMEM((2, 64, cols // 4), f32),
+            pltpu.VMEM((64, cols // 4), f32),
+            pltpu.VMEM((n, per // 2, LANES), f32),
+            pltpu.VMEM((n, per // 2, LANES), f32),
+            dma((n,)), dma((n,)), dma((6,)), dma((6,)), dma, dma, dma, dma, dma((n,)), dma((n,)),
         ],
         compiler_params=pltpu.CompilerParams(
-            collective_id=0, has_side_effects=True, vmem_limit_bytes=40 << 20
+            collective_id=0, has_side_effects=True, vmem_limit_bytes=48 << 20
         ),
-        cost_estimate=pl.CostEstimate(flops=10**9, bytes_accessed=4 << 20, transcendentals=0),
+        cost_estimate=pl.CostEstimate(flops=10**9, bytes_accessed=4 << 20, transcendentals=10**6),
     )(*args)
-
-
-def sweep_kernel(n, levels, pooled, memb, opacity, emission, sunshine, slots_out, state, trans, net):
-    rows = -(-(levels + 3) // 8) * 8
-    gpoints = emission.shape[0]
-    strata = opacity.shape[2]
-    rads = pooled.shape[2]
-    cols = memb.shape[1]
-    for h in range(2):
-        state[h, 0:LANES, :] = pooled[h, 0].T
-        state[h, LANES : 2 * LANES, :] = pooled[h, 1].T
-        tail = pooled[h, 2].T
-        state[h, 2 * LANES :, :] = tail[0:32] + tail[32:64] + tail[64:96] + tail[96:128]
-
-    def row(field, level):
-        at = field * rows + level % levels
-        return state[level // levels, at : at + 1, :]
-
-    ground = state[0, levels : levels + 1, :]
-    incline = state[0, levels + 1 : levels + 2, :]
-    incoming = state[0, levels + 2 : levels + 3, :]
-    share = jnp.broadcast_to(emission[...], (gpoints, rads))
-    slant = -1.0 / incline
-
-    def gsum(value):
-        return jnp.sum(value.reshape(gpoints // 8, 8, rads), axis=0)
-
-    def fourth(value):
-        square = value * value
-        return square * square
-
-    thermal = jnp.zeros((gpoints, rads), jnp.float32)
-    direct = sunshine[...] * incoming
-    net[0] = gsum(direct)
-    for level in range(strata):
-        tau = opacity[0, :, level : level + 1] * row(2, level)
-        for s in range(1, opacity.shape[0]):
-            tau = tau + opacity[s, :, level : level + 1] * row(2 + s, level)
-        transmit = jnp.exp(-DIFFUSE * tau)
-        trans[level] = transmit
-        source = share * fourth(row(0, level))
-        thermal = source + transmit * (thermal - source)
-        direct = direct * jnp.exp(tau * slant)
-        net[level + 1] = gsum(thermal + direct)
-    upward = share * fourth(ground)
-    net[strata] = net[strata] - gsum(upward)
-    for level in range(strata - 1, -1, -1):
-        source = share * fourth(row(0, level))
-        upward = source + trans[level] * (upward - source)
-        net[level] = net[level] - gsum(upward)
-
-    member = one_hot(iota((rads, cols), 0) == lax.shift_right_logical(memb[...], 2))
-    per = cols // n
-    fold = per // 2
-    half_lane = iota((n, fold, LANES), 2) // 64
-    fill = jnp.zeros((64 - levels, rads), jnp.float32)
-    for h in range(2):
-        change = net[h * levels : (h + 1) * levels] - net[h * levels + 1 : (h + 1) * levels + 1]
-        heat = jnp.sum(change, axis=1) / state[h, rows : rows + levels, :]
-        heat = jnp.concatenate([heat, fill], axis=0)
-        hi, lo = halves(jnp.concatenate([heat, heat], axis=0))
-        spread = (mm(hi, member) + mm(lo, member)).T.reshape(n, 2, fold, LANES)
-        slots_out[h] = jnp.where(half_lane == 0, spread[:, 0], spread[:, 1])
-
-
-def sweep(n, levels, pooled, memb, opacity, emission, sunshine):
-    rows = -(-(levels + 3) // 8) * 8
-    gpoints = emission.shape[0]
-    strata = opacity.shape[2]
-    rads = pooled.shape[2]
-    per = memb.shape[1] // n
-    f32 = jnp.float32
-    return pl.pallas_call(
-        functools.partial(sweep_kernel, n, levels),
-        out_shape=jax.ShapeDtypeStruct((2, n, per // 2, LANES), f32),
-        in_specs=[VMEM] * 5,
-        out_specs=VMEM,
-        scratch_shapes=[
-            pltpu.VMEM((2, 6 * rows, rads), f32),
-            pltpu.VMEM((strata, gpoints, rads), f32),
-            pltpu.VMEM((strata + 1, 8, rads), f32),
-        ],
-        compiler_params=pltpu.CompilerParams(vmem_limit_bytes=40 << 20),
-        cost_estimate=pl.CostEstimate(flops=2 * 10**7, bytes_accessed=1 << 20, transcendentals=10**6),
-    )(pooled, memb, opacity, emission, sunshine)
-
-
-def return_kernel(n, slots, out, other, send, recv, s_sem, r_sem, out_sem, in_sem):
-    me, side = greet(n)
-    copy = remote(slots.at[1 - side], other, s_sem, r_sem, {"sec": 1 - side})
-    copy.start()
-    copy.wait()
-    send[...] = slots[side] + other[...]
-    copies = []
-    for d in range(1, n):
-        peer = lax.rem(me + d, n)
-        copy = remote(send.at[peer], recv.at[me], out_sem.at[d], in_sem.at[d], {"grp": peer})
-        copy.start()
-        copies.append(copy)
-    recv[me] = send[me]
-    for copy in copies:
-        copy.wait()
-    out[...] = recv[...]
-
-
-def give_back(n, slots):
-    shape = slots.shape[1:]
-    f32 = jnp.float32
-    dma = pltpu.SemaphoreType.DMA
-    return pl.pallas_call(
-        functools.partial(return_kernel, n),
-        out_shape=jax.ShapeDtypeStruct(shape, f32),
-        in_specs=[VMEM],
-        out_specs=VMEM,
-        scratch_shapes=[
-            pltpu.VMEM(shape, f32), pltpu.VMEM(shape, f32), pltpu.VMEM(shape, f32),
-            dma, dma, dma((n,)), dma((n,)),
-        ],
-        compiler_params=pltpu.CompilerParams(collective_id=1, has_side_effects=True),
-        cost_estimate=pl.CostEstimate(flops=10**5, bytes_accessed=1 << 20, transcendentals=0),
-    )(slots)
-
-
-def unpack_kernel(n, returned, pos, heating):
-    levels, cols = heating.shape
-    fold = returned.shape[1]
-    value = returned[...].reshape(n * fold, LANES).T
-    place = iota((n * fold, cols), 0)
-    place = (place // fold) * (2 * fold) + lax.rem(place, fold)
-    total = None
-    for q in range(2):
-        hot = one_hot(place + q * fold == pos[...])
-        hi, lo = halves(value[64 * q : 64 * (q + 1)])
-        part = mm(hi, hot) + mm(lo, hot)
-        total = part if total is None else total + part
-    heating[...] = total[0:levels]
-
-
-def unpack(n, levels, returned, pos):
-    return pl.pallas_call(
-        functools.partial(unpack_kernel, n),
-        out_shape=jax.ShapeDtypeStruct((levels, pos.shape[1]), jnp.float32),
-        in_specs=[VMEM] * 2,
-        out_specs=VMEM,
-        compiler_params=pltpu.CompilerParams(vmem_limit_bytes=32 << 20),
-        cost_estimate=pl.CostEstimate(flops=10**8, bytes_accessed=1 << 20, transcendentals=0),
-    )(returned, pos)
 
 
 def folds_evenly(n, sides, levels, cols, species, gpoints):
@@ -563,7 +520,7 @@
     return (
         n > 3 and n % 4 == 0 and sides == 2 and species == 4
         and cols == n * 32 and cols == 4 * LANES and 2 * STEPS * HALO == cols
-        and 6 * rows == 2 * LANES + 32 and gpoints % 8 == 0
+        and 6 * rows == 2 * LANES + 32 and gpoints % 8 == 0 and 2 * levels % LEVEL_BLOCK == 0
     )
 
 
@@ -574,12 +531,10 @@
     gpoints = emission.shape[0]
     if not folds_evenly(n, lax.axis_size("sec"), levels, cols, absorb.shape[0], gpoints):
         return plain_device(*args)
-    mixed, pooled = dispatch(
-        n, warmth, depth, absorb, ground[None], sun[None], mask[None], pos, memb, adj, blend
-    )
-    slots = sweep(n, levels, pooled, memb, opacity, emission[:, None], sunshine[:, None])
-    returned = give_back(n, slots)
-    return (unpack(n, levels, returned, pos), mixed)
+    return one_kernel(
+        n, warmth, depth, absorb, ground[None], sun[None], mask[None], pos, memb, adj, blend,
+        opacity, emission[None], sunshine[None],
+    )
 
 
 def solution(mesh):

time: 51.2 us -> 43.9 us (0.86)
  Pallas kernels: 44.3 us -> 40 us
  local copies, waits for them, and re-layouts: 5.92 us -> 2.91 us
    pallas_call x4 -> x1, Pallas kernels: 44.3 us -> 40 us  [one_kernel(): pl.pallas_call(functools.partial(device_kernel, n), out_shape=(jax.ShapeD...]
    unnamed x30 -> x26, local copies, waits for them, and re-layouts: 5.73 us -> 1.94 us
    pallas_call x0 -> x1, local copies, waits for them, and re-layouts: none -> 0.98 us  [one_kernel(): pl.pallas_call(functools.partial(device_kernel, n), out_shape=(jax.ShapeD...]
where the time goes in v2:
time: 43.9 us; the launch traced here: 43.7 us
  Pallas kernels  40 us (91%)
  local copies, waits for them, and re-layouts  2.91 us (7%)
  between operations  0.84 us (2%)
    pallas_call x1, Pallas kernels, one_kernel(): pl.pallas_call(functools.partial(device_kernel, n), out_shape=(jax.ShapeD...  40 us
    unnamed x26, local copies, waits for them, and re-layouts  1.94 us
    pallas_call x1, local copies, waits for them, and re-layouts, one_kernel(): pl.pallas_call(functools.partial(device_kernel, n), out_shape=(jax.ShapeD...  0.98 us

profile of v2, /device:TPU:0, one launch (start us, length us, event | category | flops | bytes accessed | tf_op | source)
XLA Modules:
  0.0 43.7 jit_solution(6333689805634278783)
XLA Ops:
  0.6 0.0 copy-start
  0.6 0.0 copy-start.1
  0.7 0.0 copy-start.2
  0.7 0.0 copy-start.3
  0.7 0.0 copy-start.4
  0.7 0.0 copy-start.5
  0.7 0.0 copy-start.6
  0.7 0.0 copy-start.7
  0.7 0.0 copy-start.8
  0.7 0.0 copy-start.9
  0.7 0.0 copy-start.10
  0.7 0.0 copy-start.11
  0.8 1.2 %copy.15.absorb = f32[4,45,512]{2,1,0:T(8,128)S(1)} copy(f32[4,45,512]{2,0,1:T(4,128)} %param.15) | data formatting | bytes 737280 | tf_op args[2]
  2.0 0.0 copy-done
  2.0 0.0 copy-done.1
  2.0 0.0 copy-done.2
  2.0 0.0 copy-done.3
  2.0 0.0 copy-done.4
  2.1 0.0 copy-done.5
  2.1 0.0 copy-done.6
  2.1 0.0 copy-done.7
  2.1 0.0 copy-done.8
  2.1 0.0 copy-done.9
  2.1 0.0 copy-done.10
  2.1 0.0 copy-done.11
  2.1 40.0 %shard_map.140 = (f32[45,512]{1,0:T(8,128)S(1)}, f32[4,45,512]{2,1,0:T(8,128)S(1)}) custom-call(f32[45,512]{1,0:T(8,128)S(1)} %copy-done.1, f32[45,512]{1,0:T(8,128)S(1)} %copy-done.2, f32[4,45,512]{2,1,0:T(8,128)S(1)} %copy.15.absorb, f32[1,512]{1,0:T(1,128)S(1)} %bitcast.5, f32[1,512]{1,0:T(1,128)S(1)} %bitcast.6, s32[1,512]{1,0:T(1,128)S(1)} %bitcast.7, ...), custom_call_target="tpu_custom_call" | custom-call | flops 1000000000 | bytes 4194304 | tf_op jit(solution)/shard_map/pallas_call | solution.py:478
  42.1 1.0 %copy.16 = f32[4,45,512]{2,0,1:T(4,128)} copy(f32[4,45,512]{2,1,0:T(8,128)S(1)} %get-tuple-element.3) | data formatting | bytes 737280 | tf_op jit(solution)/shard_map/pallas_call | solution.py:478
  43.1 0.6 %copy.18 = f32[45,512]{1,0:T(8,128)} copy(f32[45,512]{1,0:T(8,128)S(1)} %get-tuple-element.6) | data formatting | bytes 184320
Async XLA Ops:
  0.6 1.4 %copy-start = (f32[4,56,90]{2,1,0:T(8,128)S(1)}, f32[4,56,90]{2,1,0:T(8,128)}, u32[]{:S(2)}) copy-start(f32[4,56,90]{2,1,0:T(8,128)} %opacity.1) | copy-start | bytes 241924
  0.6 1.4 %copy-start.1 = (f32[45,512]{1,0:T(8,128)S(1)}, f32[45,512]{1,0:T(8,128)}, u32[]{:S(2)}) copy-start(f32[45,512]{1,0:T(8,128)} %temp.1) | copy-start | bytes 276484
  0.7 1.4 %copy-start.2 = (f32[45,512]{1,0:T(8,128)S(1)}, f32[45,512]{1,0:T(8,128)}, u32[]{:S(2)}) copy-start(f32[45,512]{1,0:T(8,128)} %depth.1) | copy-start | bytes 276484
  0.7 1.4 %copy-start.3 = (s32[6,512]{1,0:T(8,128)S(1)}, s32[6,512]{1,0:T(8,128)}, u32[]{:S(2)}) copy-start(s32[6,512]{1,0:T(8,128)} %adj.1) | copy-start | bytes 36868
  0.7 1.4 %copy-start.4 = (f32[6,512]{1,0:T(8,128)S(1)}, f32[6,512]{1,0:T(8,128)}, u32[]{:S(2)}) copy-start(f32[6,512]{1,0:T(8,128)} %blend.1) | copy-start | bytes 36868
  0.7 1.4 %copy-start.5 = (f32[512]{0:T(512)S(1)}, f32[512]{0:T(512)}, u32[]{:S(2)}) copy-start(f32[512]{0:T(512)} %param.16) | copy-start | bytes 6148
  0.7 1.4 %copy-start.6 = (f32[512]{0:T(512)S(1)}, f32[512]{0:T(512)}, u32[]{:S(2)}) copy-start(f32[512]{0:T(512)} %param.17) | copy-start | bytes 6148
  0.7 1.4 %copy-start.7 = (s32[512]{0:T(512)S(1)}, s32[512]{0:T(512)}, u32[]{:S(2)}) copy-start(s32[512]{0:T(512)} %param.18) | copy-start | bytes 6148
  0.7 1.4 %copy-start.8 = (s32[1,512]{1,0:T(1,128)S(1)}, s32[1,512]{1,0:T(1,128)}, u32[]{:S(2)}) copy-start(s32[1,512]{1,0:T(1,128)} %pos.1) | copy-start | bytes 6148
  0.7 1.4 %copy-start.9 = (s32[1,512]{1,0:T(1,128)S(1)}, s32[1,512]{1,0:T(1,128)}, u32[]{:S(2)}) copy-start(s32[1,512]{1,0:T(1,128)} %memb.1) | copy-start | bytes 6148
  0.7 1.4 %copy-start.10 = (f32[56]{0:T(128)S(1)}, f32[56]{0:T(128)}, u32[]{:S(2)}) copy-start(f32[56]{0:T(128)} %param.24) | copy-start | bytes 676
  0.7 1.4 %copy-start.11 = (f32[56]{0:T(128)S(1)}, f32[56]{0:T(128)}, u32[]{:S(2)}) copy-start(f32[56]{0:T(128)} %param.25) | copy-start | bytes 676

commit v3 on v2

--- a/solution.py
+++ b/solution.py
@@ -222,15 +222,22 @@
     return lax.dot_general(left, right, dims, preferred_element_type=jnp.float32)
 
 
+def flipped(me, distance):
+    peer, bit = me, 1
+    while bit <= distance:
+        if distance & bit:
+            peer = peer + bit - 2 * bit * lax.rem(me // bit, 2)
+        bit *= 2
+    return peer
+
+
 def greet(n):
     me, side = lax.axis_index("grp"), lax.axis_index("sec")
     barrier = pltpu.get_barrier_semaphore()
-    for d in range(1, n):
-        peer = lax.rem(me + d, n)
-        pl.semaphore_signal(barrier, inc=1, device_id={"grp": peer}, device_id_type=MESH)
+    for d in range(n - 1, 0, -1):
+        pl.semaphore_signal(barrier, inc=1, device_id={"grp": flipped(me, d)}, device_id_type=MESH)
     pl.semaphore_signal(barrier, inc=1, device_id={"sec": 1 - side}, device_id_type=MESH)
-    pl.semaphore_wait(barrier, n)
-    return me, side
+    return me, side, barrier
 
 
 def remote(src, dst, send_sem, recv_sem, device):
@@ -254,7 +261,7 @@
     pack = per // 4
     rads = cols // 4
     wide = STEPS * HALO
-    me, side = greet(n)
+    me, side, barrier = greet(n)
     right, left = lax.rem(me + 1, n), lax.rem(me + n - 1, n)
 
     halo = []
@@ -265,8 +272,6 @@
         first, last = src.at[lead + (pl.ds(0, wide),)], src.at[lead + (pl.ds(cols - wide, wide),)]
         halo.append(remote(first, to_left, hs_sem.at[2 * k], hr_sem.at[2 * k], {"grp": left}))
         halo.append(remote(last, to_right, hs_sem.at[2 * k + 1], hr_sem.at[2 * k + 1], {"grp": right}))
-    for copy in halo:
-        copy.start()
 
     data[...] = jnp.zeros_like(data)
     data[0:levels, :] = temp[...]
@@ -280,13 +285,13 @@
     for q in range(1, 4):
         data[2 * LANES + 32 * q : 2 * LANES + 32 * (q + 1), :] = rest
     data_hi, data_lo = halves(data[...])
-    relative = pos[...] - me * per
-    relative = jnp.where(relative < 0, relative + cols, relative)
-    chunk = 4 * per
     lane_block = iota((4, pack, LANES), 2) // 32
+    slot_row = iota((per, cols), 0) - pos[...]
+    order = [*range(n // 8, n // 4), *range(n // 8 - 1, -1, -1)]
     copies = []
-    for c in range(n // 4):
-        hot = one_hot(iota((chunk, cols), 0) + c * chunk == relative)
+    for turn, c in enumerate(order):
+        peers = [flipped(me, d) for d in range(4 * c, 4 * c + 4)]
+        hot = jnp.concatenate([one_hot(slot_row + peer * per == 0) for peer in peers], axis=0)
         out = mm(hot, data_hi, NT) + mm(hot, data_lo, NT)
         send[4 * c : 4 * c + 4, 0:per, :] = out[:, 0:LANES].reshape(4, per, LANES)
         send[4 * c : 4 * c + 4, per : 2 * per, :] = out[:, LANES : 2 * LANES].reshape(4, per, LANES)
@@ -295,12 +300,17 @@
         for q in range(1, 4):
             folded = jnp.where(lane_block == q, tail[:, q], folded)
         send[4 * c : 4 * c + 4, 2 * per :, :] = folded
+        if turn == 0:
+            pl.semaphore_wait(barrier, n)
         for d in range(max(4 * c, 1), 4 * c + 4):
             copy = remote(
-                send.at[d], recv.at[me], out_sem.at[d], in_sem.at[d], {"grp": lax.rem(me + d, n)}
+                send.at[d], recv.at[me], out_sem.at[d], in_sem.at[d], {"grp": peers[d - 4 * c]}
             )
             copy.start()
             copies.append(copy)
+        if turn == 0:
+            for copy in halo:
+                copy.start()
     recv[me] = send[0]
 
     grid_a[...] = jnp.zeros_like(grid_a)
@@ -372,20 +382,28 @@
     big_block = iota((n, pack, LANES), 2) // 32
     tail = jnp.stack([jnp.where(big_block == q, tail, 0.0) for q in range(4)], axis=1)
     parts.append(tail.reshape(cols, LANES))
+    across = []
     for k, part in enumerate(parts):
         hi, lo = halves(part)
         pooled[side, k] = (mm(member, hi) + mm(member, lo)) * 0.25
-    copy = remote(pooled.at[side], pooled.at[side], ps_sem, pr_sem, {"sec": 1 - side})
-    copy.start()
-    copy.wait()
-
-    for h in range(2):
+        copy = remote(
+            pooled.at[side, k], pooled.at[side, k], ps_sem.at[k], pr_sem.at[k], {"sec": 1 - side}
+        )
+        copy.start()
+        across.append(copy)
+
+    def unfold(h):
         tail = pooled[h, 2].T
         tail = tail[0:32] + tail[32:64] + tail[64:96] + tail[96:128]
         field = jnp.concatenate([pooled[h, 0].T, pooled[h, 1].T, tail], axis=0)
         for k in range(2 + species):
-            state[k, h * levels : (h + 1) * levels, :] = field[k * rows : k * rows + levels]
-        surface = field[levels : levels + 3]
+            state[k, h, 0:levels, :] = field[k * rows : k * rows + levels]
+        return field[levels : levels + 3]
+
+    surface = unfold(side)
+    for copy in across:
+        copy.wait()
+    unfold(1 - side)
 
     def fourth(value):
         square = value * value
@@ -395,20 +413,21 @@
         return jnp.sum(value.reshape(gpoints // 8, 8, rads), axis=0)
 
     slant = -1.0 / surface[1:2]
-    state[0, 0:strata, :] = fourth(state[0, 0:strata, :])
+    state[0, :, 0:levels, :] = fourth(state[0, :, 0:levels, :])
 
     def down(b, fluxes):
         thermal, direct = fluxes
         coeffs = opac[b]
         for i in range(LEVEL_BLOCK):
             level = b * LEVEL_BLOCK + i
+            half = level // levels
             tau = None
             for k in range(species):
-                part = coeffs[k * gpoints : (k + 1) * gpoints, i : i + 1] * state[2 + k, pl.ds(level, 1), :]
+                part = coeffs[k * gpoints : (k + 1) * gpoints, i : i + 1] * state[2 + k, half, pl.ds(level - half * levels, 1), :]
                 tau = part if tau is None else tau + part
             transmit = jnp.exp(-DIFFUSE * tau)
             trans[level] = transmit
-            source = share * state[0, pl.ds(level, 1), :]
+            source = share * state[0, half, pl.ds(level - half * levels, 1), :]
             thermal = source + transmit * (thermal - source)
             direct = direct * jnp.exp(tau * slant)
             net[level + 1] = gsum(thermal + direct)
@@ -423,7 +442,8 @@
     def up(b, upward):
         for i in range(LEVEL_BLOCK):
             level = strata - 1 - (b * LEVEL_BLOCK + i)
-            source = share * state[0, pl.ds(level, 1), :]
+            half = level // levels
+            source = share * state[0, half, pl.ds(level - half * levels, 1), :]
             upward = source + trans[level] * (upward - source)
             net[level] = net[level] - gsum(upward)
         return upward
@@ -432,7 +452,7 @@
     heat[...] = jnp.zeros_like(heat)
     for h in range(2):
         change = net[h * levels : (h + 1) * levels] - net[h * levels + 1 : (h + 1) * levels + 1]
-        heat[h, 0:levels] = jnp.sum(change, axis=1) / state[1, h * levels : (h + 1) * levels, :]
+        heat[h, 0:levels] = jnp.sum(change, axis=1) / state[1, h, 0:levels, :]
     copy = remote(heat.at[1 - side], other, ts_sem, tr_sem, {"sec": 1 - side})
     copy.start()
     copy.wait()
@@ -442,8 +462,8 @@
     spread = (mm(hi, member) + mm(lo, member)).T.reshape(n, 2, fold, LANES)
     back[...] = jnp.where(iota((n, fold, LANES), 2) // 64 == 0, spread[:, 0], spread[:, 1])
     copies = []
-    for d in range(1, n):
-        peer = lax.rem(me + d, n)
+    for d in [*range(n // 2, n), *range(n // 2 - 1, 0, -1)]:
+        peer = flipped(me, d)
         copy = remote(back.at[peer], home.at[me], bo_sem.at[d], bi_sem.at[d], {"grp": peer})
         copy.start()
         copies.append(copy)
@@ -498,7 +518,7 @@
             pltpu.VMEM((span // 256, 512, 256), jnp.bfloat16),
             pltpu.VMEM((span // 256, 512, 256), jnp.bfloat16),
             pltpu.VMEM((2, 3, cols // 4, LANES), f32),
-            pltpu.VMEM((2 + species, -(-strata // 8) * 8, cols // 4), f32),
+            pltpu.VMEM((2 + species, 2, rows, cols // 4), f32),
             pltpu.VMEM((strata // LEVEL_BLOCK, species * gpoints, LANES), f32),
             pltpu.VMEM((strata, gpoints, cols // 4), f32),
             pltpu.VMEM((strata + 1, 8, cols // 4), f32),
@@ -506,7 +526,7 @@
             pltpu.VMEM((64, cols // 4), f32),
             pltpu.VMEM((n, per // 2, LANES), f32),
             pltpu.VMEM((n, per // 2, LANES), f32),
-            dma((n,)), dma((n,)), dma((6,)), dma((6,)), dma, dma, dma, dma, dma((n,)), dma((n,)),
+            dma((n,)), dma((n,)), dma((6,)), dma((6,)), dma((3,)), dma((3,)), dma, dma, dma((n,)), dma((n,)),
         ],
         compiler_params=pltpu.CompilerParams(
             collective_id=0, has_side_effects=True, vmem_limit_bytes=48 << 20
@@ -518,7 +538,7 @@
 def folds_evenly(n, sides, levels, cols, species, gpoints):
     rows = -(-(levels + 3) // 8) * 8
     return (
-        n > 3 and n % 4 == 0 and sides == 2 and species == 4
+        n > 7 and n & (n - 1) == 0 and sides == 2 and species == 4
         and cols == n * 32 and cols == 4 * LANES and 2 * STEPS * HALO == cols
         and 6 * rows == 2 * LANES + 32 and gpoints % 8 == 0 and 2 * levels % LEVEL_BLOCK == 0
     )

time: 43.9 us -> 43.8 us (level)
  no operation moved by 1% of the time
where the time goes in v3:
time: 43.8 us; the launch traced here: 43.6 us
  Pallas kernels  39.9 us (91%)
  local copies, waits for them, and re-layouts  2.91 us (7%)
  between operations  0.84 us (2%)
    pallas_call x1, Pallas kernels, one_kernel(): pl.pallas_call(functools.partial(device_kernel, n), out_shape=(jax.ShapeD...  39.9 us
    unnamed x26, local copies, waits for them, and re-layouts  1.94 us
    pallas_call x1, local copies, waits for them, and re-layouts, one_kernel(): pl.pallas_call(functools.partial(device_kernel, n), out_shape=(jax.ShapeD...  0.98 us

profile of v3, /device:TPU:0, one launch (start us, length us, event | category | flops | bytes accessed | tf_op | source)
XLA Modules:
  0.0 43.6 jit_solution(5476415858656487714)
XLA Ops:
  0.6 0.0 copy-start
  0.6 0.0 copy-start.1
  0.7 0.0 copy-start.2
  0.7 0.0 copy-start.3
  0.7 0.0 copy-start.4
  0.7 0.0 copy-start.5
  0.7 0.0 copy-start.6
  0.7 0.0 copy-start.7
  0.7 0.0 copy-start.8
  0.7 0.0 copy-start.9
  0.7 0.0 copy-start.10
  0.7 0.0 copy-start.11
  0.8 1.2 %copy.15.absorb = f32[4,45,512]{2,1,0:T(8,128)S(1)} copy(f32[4,45,512]{2,0,1:T(4,128)} %param.15) | data formatting | bytes 737280 | tf_op args[2]
  2.0 0.0 copy-done
  2.0 0.0 copy-done.1
  2.0 0.0 copy-done.2
  2.0 0.0 copy-done.3
  2.0 0.0 copy-done.4
  2.1 0.0 copy-done.5
  2.1 0.0 copy-done.6
  2.1 0.0 copy-done.7
  2.1 0.0 copy-done.8
  2.1 0.0 copy-done.9
  2.1 0.0 copy-done.10
  2.1 0.0 copy-done.11
  2.1 39.9 %shard_map.140 = (f32[45,512]{1,0:T(8,128)S(1)}, f32[4,45,512]{2,1,0:T(8,128)S(1)}) custom-call(f32[45,512]{1,0:T(8,128)S(1)} %copy-done.1, f32[45,512]{1,0:T(8,128)S(1)} %copy-done.2, f32[4,45,512]{2,1,0:T(8,128)S(1)} %copy.15.absorb, f32[1,512]{1,0:T(1,128)S(1)} %bitcast.5, f32[1,512]{1,0:T(1,128)S(1)} %bitcast.6, s32[1,512]{1,0:T(1,128)S(1)} %bitcast.7, ...), custom_call_target="tpu_custom_call" | custom-call | flops 1000000000 | bytes 4194304 | tf_op jit(solution)/shard_map/pallas_call | solution.py:498
  42.0 1.0 %copy.16 = f32[4,45,512]{2,0,1:T(4,128)} copy(f32[4,45,512]{2,1,0:T(8,128)S(1)} %get-tuple-element.3) | data formatting | bytes 737280 | tf_op jit(solution)/shard_map/pallas_call | solution.py:498
  43.0 0.6 %copy.18 = f32[45,512]{1,0:T(8,128)} copy(f32[45,512]{1,0:T(8,128)S(1)} %get-tuple-element.6) | data formatting | bytes 184320
Async XLA Ops:
  0.6 1.4 %copy-start = (f32[4,56,90]{2,1,0:T(8,128)S(1)}, f32[4,56,90]{2,1,0:T(8,128)}, u32[]{:S(2)}) copy-start(f32[4,56,90]{2,1,0:T(8,128)} %opacity.1) | copy-start | bytes 241924
  0.6 1.4 %copy-start.1 = (f32[45,512]{1,0:T(8,128)S(1)}, f32[45,512]{1,0:T(8,128)}, u32[]{:S(2)}) copy-start(f32[45,512]{1,0:T(8,128)} %temp.1) | copy-start | bytes 276484
  0.7 1.4 %copy-start.2 = (f32[45,512]{1,0:T(8,128)S(1)}, f32[45,512]{1,0:T(8,128)}, u32[]{:S(2)}) copy-start(f32[45,512]{1,0:T(8,128)} %depth.1) | copy-start | bytes 276484
  0.7 1.4 %copy-start.3 = (s32[6,512]{1,0:T(8,128)S(1)}, s32[6,512]{1,0:T(8,128)}, u32[]{:S(2)}) copy-start(s32[6,512]{1,0:T(8,128)} %adj.1) | copy-start | bytes 36868
  0.7 1.4 %copy-start.4 = (f32[6,512]{1,0:T(8,128)S(1)}, f32[6,512]{1,0:T(8,128)}, u32[]{:S(2)}) copy-start(f32[6,512]{1,0:T(8,128)} %blend.1) | copy-start | bytes 36868
  0.7 1.4 %copy-start.5 = (f32[512]{0:T(512)S(1)}, f32[512]{0:T(512)}, u32[]{:S(2)}) copy-start(f32[512]{0:T(512)} %param.16) | copy-start | bytes 6148
  0.7 1.4 %copy-start.6 = (f32[512]{0:T(512)S(1)}, f32[512]{0:T(512)}, u32[]{:S(2)}) copy-start(f32[512]{0:T(512)} %param.17) | copy-start | bytes 6148
  0.7 1.4 %copy-start.7 = (s32[512]{0:T(512)S(1)}, s32[512]{0:T(512)}, u32[]{:S(2)}) copy-start(s32[512]{0:T(512)} %param.18) | copy-start | bytes 6148
  0.7 1.4 %copy-start.8 = (s32[1,512]{1,0:T(1,128)S(1)}, s32[1,512]{1,0:T(1,128)}, u32[]{:S(2)}) copy-start(s32[1,512]{1,0:T(1,128)} %pos.1) | copy-start | bytes 6148
  0.7 1.4 %copy-start.9 = (s32[1,512]{1,0:T(1,128)S(1)}, s32[1,512]{1,0:T(1,128)}, u32[]{:S(2)}) copy-start(s32[1,512]{1,0:T(1,128)} %memb.1) | copy-start | bytes 6148
  0.7 1.4 %copy-start.10 = (f32[56]{0:T(128)S(1)}, f32[56]{0:T(128)}, u32[]{:S(2)}) copy-start(f32[56]{0:T(128)} %param.24) | copy-start | bytes 676
  0.7 1.4 %copy-start.11 = (f32[56]{0:T(128)S(1)}, f32[56]{0:T(128)}, u32[]{:S(2)}) copy-start(f32[56]{0:T(128)} %param.25) | copy-start | bytes 676

commit v4 on v3

--- a/solution.py
+++ b/solution.py
@@ -252,7 +252,7 @@
     opacity, emission, sunshine, heating, mixed_out,
     data, send, recv, halo_l, halo_r, adj_l, adj_r, blend_l, blend_r,
     grid_a, grid_b, mix_hi, mix_lo, pooled,
-    state, opac, trans, net, heat, other, back, home,
+    state, opac, trans, net, heat, other, back, home, pair,
     out_sem, in_sem, hs_sem, hr_sem, ps_sem, pr_sem, ts_sem, tr_sem, bo_sem, bi_sem,
 ):
     species, levels, cols = absorb.shape
@@ -344,22 +344,28 @@
         hi, lo = halves(matrix)
         mix_hi[b, 0 : high - low, :] = hi
         mix_lo[b, 0 : high - low, :] = lo
-    old, new = grid_a, grid_b
-    for step in range(STEPS):
+    lines = species * rows
+
+    def mix(step):
+        old, new = (grid_a, grid_b) if step % 2 == 0 else (grid_b, grid_a)
+        hi, lo = halves(old[...])
+        pair[0:lines, :] = hi
+        pair[lines:, :] = lo
         blocks = range(span // width)
         if step == STEPS - 1:
             blocks = range(wide // width, (wide + cols) // width)
         for b in blocks:
             low, high = windows[b]
             here = slice(width * b, width * (b + 1))
-            hi, lo = halves(old[:, low:high])
-            left_hi = mix_hi[b, 0 : high - low, :]
-            update = mm(hi, left_hi) + mm(lo, left_hi) + mm(hi, mix_lo[b, 0 : high - low, :])
+            both = mm(pair[:, low:high], mix_hi[b, 0 : high - low, :])
+            update = both[0:lines] + both[lines:]
+            update = update + mm(pair[0:lines, low:high], mix_lo[b, 0 : high - low, :])
             centre = old[:, here]
             new[:, here] = centre + (update - total[:, here] * centre)
-        old, new = new, old
-    for s in range(species):
-        mixed_out[s] = old[s * rows : s * rows + levels, wide : wide + cols]
+        return new
+
+    for step in range(STEPS - 1):
+        mix(step)
 
     gpoints = emission.shape[1]
     strata = opacity.shape[2]
@@ -471,16 +477,19 @@
     place = iota((n * fold, cols), 0)
     place = (place // fold) * (2 * fold) + lax.rem(place, fold) - pos[...]
     hots = [one_hot(place + q * fold == 0) for q in range(2)]
+    last = mix(STEPS - 1)
+    for s in range(species):
+        mixed_out[s] = last[s * rows : s * rows + levels, wide : wide + cols]
     for copy in copies:
         copy.wait()
     value = home[...].reshape(n * fold, LANES).T
     hi, lo = halves(value)
-    total = None
+    heats = None
     for q in range(2):
         here = slice(64 * q, 64 * (q + 1))
         part = mm(hi[here], hots[q]) + mm(lo[here], hots[q])
-        total = part if total is None else total + part
-    heating[...] = total[0:levels]
+        heats = part if heats is None else heats + part
+    heating[...] = heats[0:levels]
 
 
 def one_kernel(n, *args):
@@ -526,6 +535,7 @@
             pltpu.VMEM((64, cols // 4), f32),
             pltpu.VMEM((n, per // 2, LANES), f32),
             pltpu.VMEM((n, per // 2, LANES), f32),
+            pltpu.VMEM((2 * species * rows, span), jnp.bfloat16),
             dma((n,)), dma((n,)), dma((6,)), dma((6,)), dma((3,)), dma((3,)), dma, dma, dma((n,)), dma((n,)),
         ],
         compiler_params=pltpu.CompilerParams(

time: 43.8 us -> 43.5 us (level)
  no operation moved by 1% of the time
where the time goes in v4:
time: 43.5 us; the launch traced here: 43.4 us
  Pallas kernels  39.6 us (91%)
  local copies, waits for them, and re-layouts  2.91 us (7%)
  between operations  0.84 us (2%)
    pallas_call x1, Pallas kernels, one_kernel(): pl.pallas_call(functools.partial(device_kernel, n), out_shape=(jax.ShapeD...  39.6 us
    unnamed x26, local copies, waits for them, and re-layouts  1.94 us
    pallas_call x1, local copies, waits for them, and re-layouts, one_kernel(): pl.pallas_call(functools.partial(device_kernel, n), out_shape=(jax.ShapeD...  0.98 us

profile of v4, /device:TPU:0, one launch (start us, length us, event | category | flops | bytes accessed | tf_op | source)
XLA Modules:
  0.0 43.4 jit_solution(5652494137374788886)
XLA Ops:
  0.6 0.0 copy-start
  0.6 0.0 copy-start.1
  0.7 0.0 copy-start.2
  0.7 0.0 copy-start.3
  0.7 0.0 copy-start.4
  0.7 0.0 copy-start.5
  0.7 0.0 copy-start.6
  0.7 0.0 copy-start.7
  0.7 0.0 copy-start.8
  0.7 0.0 copy-start.9
  0.7 0.0 copy-start.10
  0.7 0.0 copy-start.11
  0.8 1.2 %copy.15.absorb = f32[4,45,512]{2,1,0:T(8,128)S(1)} copy(f32[4,45,512]{2,0,1:T(4,128)} %param.15) | data formatting | bytes 737280 | tf_op args[2]
  2.0 0.0 copy-done
  2.0 0.0 copy-done.1
  2.0 0.0 copy-done.2
  2.0 0.0 copy-done.3
  2.0 0.0 copy-done.4
  2.1 0.0 copy-done.5
  2.1 0.0 copy-done.6
  2.1 0.0 copy-done.7
  2.1 0.0 copy-done.8
  2.1 0.0 copy-done.9
  2.1 0.0 copy-done.10
  2.1 0.0 copy-done.11
  2.1 39.6 %shard_map.140 = (f32[45,512]{1,0:T(8,128)S(1)}, f32[4,45,512]{2,1,0:T(8,128)S(1)}) custom-call(f32[45,512]{1,0:T(8,128)S(1)} %copy-done.1, f32[45,512]{1,0:T(8,128)S(1)} %copy-done.2, f32[4,45,512]{2,1,0:T(8,128)S(1)} %copy.15.absorb, f32[1,512]{1,0:T(1,128)S(1)} %bitcast.5, f32[1,512]{1,0:T(1,128)S(1)} %bitcast.6, s32[1,512]{1,0:T(1,128)S(1)} %bitcast.7, ...), custom_call_target="tpu_custom_call" | custom-call | flops 1000000000 | bytes 4194304 | tf_op jit(solution)/shard_map/pallas_call | solution.py:507
  41.8 1.0 %copy.16 = f32[4,45,512]{2,0,1:T(4,128)} copy(f32[4,45,512]{2,1,0:T(8,128)S(1)} %get-tuple-element.3) | data formatting | bytes 737280 | tf_op jit(solution)/shard_map/pallas_call | solution.py:507
  42.7 0.6 %copy.18 = f32[45,512]{1,0:T(8,128)} copy(f32[45,512]{1,0:T(8,128)S(1)} %get-tuple-element.6) | data formatting | bytes 184320
Async XLA Ops:
  0.6 1.4 %copy-start = (f32[4,56,90]{2,1,0:T(8,128)S(1)}, f32[4,56,90]{2,1,0:T(8,128)}, u32[]{:S(2)}) copy-start(f32[4,56,90]{2,1,0:T(8,128)} %opacity.1) | copy-start | bytes 241924
  0.6 1.4 %copy-start.1 = (f32[45,512]{1,0:T(8,128)S(1)}, f32[45,512]{1,0:T(8,128)}, u32[]{:S(2)}) copy-start(f32[45,512]{1,0:T(8,128)} %temp.1) | copy-start | bytes 276484
  0.7 1.4 %copy-start.2 = (f32[45,512]{1,0:T(8,128)S(1)}, f32[45,512]{1,0:T(8,128)}, u32[]{:S(2)}) copy-start(f32[45,512]{1,0:T(8,128)} %depth.1) | copy-start | bytes 276484
  0.7 1.4 %copy-start.3 = (s32[6,512]{1,0:T(8,128)S(1)}, s32[6,512]{1,0:T(8,128)}, u32[]{:S(2)}) copy-start(s32[6,512]{1,0:T(8,128)} %adj.1) | copy-start | bytes 36868
  0.7 1.4 %copy-start.4 = (f32[6,512]{1,0:T(8,128)S(1)}, f32[6,512]{1,0:T(8,128)}, u32[]{:S(2)}) copy-start(f32[6,512]{1,0:T(8,128)} %blend.1) | copy-start | bytes 36868
  0.7 1.4 %copy-start.5 = (f32[512]{0:T(512)S(1)}, f32[512]{0:T(512)}, u32[]{:S(2)}) copy-start(f32[512]{0:T(512)} %param.16) | copy-start | bytes 6148
  0.7 1.4 %copy-start.6 = (f32[512]{0:T(512)S(1)}, f32[512]{0:T(512)}, u32[]{:S(2)}) copy-start(f32[512]{0:T(512)} %param.17) | copy-start | bytes 6148
  0.7 1.4 %copy-start.7 = (s32[512]{0:T(512)S(1)}, s32[512]{0:T(512)}, u32[]{:S(2)}) copy-start(s32[512]{0:T(512)} %param.18) | copy-start | bytes 6148
  0.7 1.4 %copy-start.8 = (s32[1,512]{1,0:T(1,128)S(1)}, s32[1,512]{1,0:T(1,128)}, u32[]{:S(2)}) copy-start(s32[1,512]{1,0:T(1,128)} %pos.1) | copy-start | bytes 6148
  0.7 1.4 %copy-start.9 = (s32[1,512]{1,0:T(1,128)S(1)}, s32[1,512]{1,0:T(1,128)}, u32[]{:S(2)}) copy-start(s32[1,512]{1,0:T(1,128)} %memb.1) | copy-start | bytes 6148
  0.7 1.4 %copy-start.10 = (f32[56]{0:T(128)S(1)}, f32[56]{0:T(128)}, u32[]{:S(2)}) copy-start(f32[56]{0:T(128)} %param.24) | copy-start | bytes 676
  0.7 1.4 %copy-start.11 = (f32[56]{0:T(128)S(1)}, f32[56]{0:T(128)}, u32[]{:S(2)}) copy-start(f32[56]{0:T(128)} %param.25) | copy-start | bytes 676
